TPU v7x, 32 devices: a whole 2x2x4 slice. The times are simulated.
32 devices in a mesh: seq: 16 (over z, y, x), dp: 2 (over core).
Axes of the slice: x: 2, y: 2, z: 4, core: 2. Of those that a mesh axis runs over, the one named last changes fastest.
Arguments:
- queries: bfloat16 [2, 4096, 1024], P('dp', 'seq'), may hold values from -1000 to 1000, as said below
- key_rows: bfloat16 [2, 4096, 1024], P('dp', 'seq'), may hold values from -1000 to 1000, as said below
- value_rows: bfloat16 [2, 4096, 1024], P('dp', 'seq'), may hold values from -6 to 6
- cotangent: bfloat16 [2, 4096, 1024], P('dp', 'seq'), may hold values from -6 to 6
- w_out: bfloat16 [1024, 1024], P('dp'), may hold values from -0.1875 to 0.1875
- cluster_ids: int32 [2, 4096], P('dp', 'seq'), may hold values from 0 to 63, as said below
Outputs:
- projected: bfloat16 [2, 4096, 1024], P('dp', 'seq')
- grad_queries: bfloat16 [2, 4096, 1024], P('dp', 'seq')
- grad_keys: bfloat16 [2, 4096, 1024], P('dp', 'seq')
- grad_values: bfloat16 [2, 4096, 1024], P('dp', 'seq')
- weight_grad: float32 [1024, 1024], P(('seq', 'dp'))
Inputs may be any that keep to these rules, and one draw needn't show every extreme that they name: `cluster_ids`: among the 256 tokens of one index of seq no cluster id occurs more than 8 times; in every sequence some cluster has exactly 8 tokens on every index of seq. `queries`: finite values. `key_rows`: finite values.
All inputs are finite; a program needn't handle non-finite values.
Results may differ from a plain program's by a relative error of at most 0.014.
Values may be sent and summed in bfloat16 or wider, within the bound.
A program may use at most 128 MiB of HBM per device.

v0:
```python
import functools
import math

import jax
import jax.numpy as jnp
from jax import lax
from jax.experimental import pallas as pl
from jax.experimental.pallas import tpu as pltpu
from jax.sharding import PartitionSpec as P

MESH = pl.DeviceIdType.MESH
HD = 128
CL_DEV = 4


EPS = 1e-06


def head_norm(matrix):
    shaped = matrix.astype(jnp.float32).reshape(matrix.shape[0], matrix.shape[1] // HD, HD)
    factor = lax.rsqrt(jnp.mean(shaped * shaped, axis=-1, keepdims=True) + EPS)
    return (shaped * factor, factor)


def norm_back(gradient, normed, factor):
    shaped = gradient.astype(jnp.float32).reshape(normed.shape)
    inner = jnp.mean(shaped * normed, axis=-1, keepdims=True)
    return (factor * (shaped - normed * inner)).reshape(normed.shape[0], -1)


def split_heads(blocks):
    return blocks.reshape(blocks.shape[0], blocks.shape[1], blocks.shape[2] // HD, HD)


def attend(q_blk, k_blk, v_blk, key_valid):
    q_four, k_four, v_four = (split_heads(q_blk), split_heads(k_blk), split_heads(v_blk))
    scores = jnp.einsum(
        "cqhd,ckhd->chqk", q_four, k_four, preferred_element_type=jnp.float32
    ) / math.sqrt(HD)
    positions = jnp.arange(q_blk.shape[1])
    below_diag = positions[None, :] <= positions[:, None]
    on_diagonal = positions[None, :] == positions[:, None]
    allowed = jnp.logical_or(
        jnp.logical_and(key_valid[:, None, None, :], below_diag[None, None]),
        on_diagonal[None, None],
    )
    weights = jnp.where(allowed, jnp.exp(scores), 0.0)
    probs = weights / jnp.sum(weights, axis=-1, keepdims=True)
    probs_b = probs.astype(jnp.bfloat16)
    attn = jnp.einsum(
        "chqk,ckhd->cqhd", probs_b, v_four, preferred_element_type=jnp.float32
    ).astype(jnp.bfloat16)
    return (attn.reshape(q_blk.shape), probs, probs_b)


def attend_back(q_blk, k_blk, v_blk, probs, probs_b, attn, d_blk):
    q_four, k_four, v_four = (split_heads(q_blk), split_heads(k_blk), split_heads(v_blk))
    d_four, a_four = (split_heads(d_blk), split_heads(attn))
    grad_value = jnp.einsum(
        "chqk,cqhd->ckhd", probs_b, d_four, preferred_element_type=jnp.float32
    ).astype(jnp.bfloat16)
    grad_prob = jnp.einsum("cqhd,ckhd->chqk", d_four, v_four, preferred_element_type=jnp.float32)
    delta_row = jnp.sum(d_four.astype(jnp.float32) * a_four.astype(jnp.float32), axis=-1)
    grad_score = (probs * (grad_prob - jnp.transpose(delta_row, (0, 2, 1))[..., None])).astype(
        jnp.bfloat16
    )
    grad_qhat = jnp.einsum(
        "chqk,ckhd->cqhd", grad_score, k_four, preferred_element_type=jnp.float32
    ) / math.sqrt(HD)
    grad_khat = jnp.einsum(
        "chqk,cqhd->ckhd", grad_score, q_four, preferred_element_type=jnp.float32
    ) / math.sqrt(HD)
    shape = q_blk.shape
    return (
        grad_qhat.astype(jnp.bfloat16).reshape(shape),
        grad_khat.astype(jnp.bfloat16).reshape(shape),
        grad_value.reshape(shape),
    )


def per_device_slots(queries, key_rows, value_rows, cotangent, w_out, cluster_ids):
    token_count = queries.shape[1]
    features = queries.shape[2]
    seq_devices = lax.axis_size("seq")
    data_devices = lax.axis_size("dp")
    capacity = 2 * token_count // (CL_DEV * seq_devices)
    total_slots = 2 * token_count
    labels = cluster_ids[0]
    positions = jnp.arange(token_count)
    matching = labels[:, None] == labels[None, :]
    earlier = positions[None, :] < positions[:, None]
    ranks = jnp.sum(jnp.logical_and(matching, earlier), axis=1)
    slot_index = labels * capacity + ranks

    def pack(matrix):
        empty = jnp.zeros((total_slots, matrix.shape[1]), matrix.dtype)
        return (
            empty.at[slot_index].set(matrix).reshape(seq_devices, CL_DEV, capacity, matrix.shape[1])
        )

    def unpack(returned):
        return returned.reshape(total_slots, -1)[slot_index]

    taken_slots = (
        jnp.zeros((total_slots,), jnp.bfloat16)
        .at[slot_index]
        .set(1.0)
        .reshape(seq_devices, CL_DEV, capacity)
    )
    q_norm, q_factor = head_norm(queries[0])
    k_norm, k_factor = head_norm(key_rows[0])
    q_hat = q_norm.reshape(token_count, features).astype(jnp.bfloat16)
    k_hat = k_norm.reshape(token_count, features).astype(jnp.bfloat16)
    cotan = cotangent[0]
    w_full = lax.all_gather(w_out, "dp", axis=0, tiled=True)
    received = (
        lax.all_to_all(pack(q_hat), "seq", split_axis=0, concat_axis=2, tiled=True),
        lax.all_to_all(pack(k_hat), "seq", split_axis=0, concat_axis=2, tiled=True),
        lax.all_to_all(pack(value_rows[0]), "seq", split_axis=0, concat_axis=2, tiled=True),
        lax.all_to_all(taken_slots, "seq", split_axis=0, concat_axis=2, tiled=True),
    )
    q_blk, k_blk, v_blk = (received[0][0], received[1][0], received[2][0])
    key_valid = received[3][0] > 0
    attn_blk, probs, probs_b = attend(q_blk, k_blk, v_blk, key_valid)
    attn_back = lax.all_to_all(attn_blk[None], "seq", split_axis=2, concat_axis=0, tiled=True)
    attn = unpack(attn_back)
    grad_attn = lax.dot_general(
        cotan, w_full, (((1,), (1,)), ((), ())), preferred_element_type=jnp.float32
    ).astype(jnp.bfloat16)
    grad_recv = lax.all_to_all(pack(grad_attn), "seq", split_axis=0, concat_axis=2, tiled=True)
    grad_qblk, grad_kblk, grad_vblk = attend_back(
        q_blk, k_blk, v_blk, probs, probs_b, attn_blk, grad_recv[0]
    )
    grads_back = (
        lax.all_to_all(grad_qblk[None], "seq", split_axis=2, concat_axis=0, tiled=True),
        lax.all_to_all(grad_kblk[None], "seq", split_axis=2, concat_axis=0, tiled=True),
        lax.all_to_all(grad_vblk[None], "seq", split_axis=2, concat_axis=0, tiled=True),
    )
    grad_qhat, grad_khat, grad_values = (
        unpack(grads_back[0]),
        unpack(grads_back[1]),
        unpack(grads_back[2]),
    )
    projected = jnp.dot(attn, w_full, preferred_element_type=jnp.float32).astype(jnp.bfloat16)
    grad_queries = norm_back(grad_qhat, q_norm, q_factor).astype(jnp.bfloat16)
    grad_keys = norm_back(grad_khat, k_norm, k_factor).astype(jnp.bfloat16)
    local_term = lax.dot_general(
        attn, cotan, (((0,), (0,)), ((), ())), preferred_element_type=jnp.float32
    )
    summed = lax.psum_scatter(local_term, ("seq", "dp"), scatter_dimension=0, tiled=True)
    weight_grad = summed / math.sqrt(token_count * seq_devices * data_devices)
    return (projected[None], grad_queries[None], grad_keys[None], grad_values[None], weight_grad)


def greet_all(seq_devices):
    barrier = pltpu.get_barrier_semaphore()
    me = lax.axis_index("seq") * 2 + lax.axis_index("dp")
    everyone = 2 * seq_devices

    def greet(step, carry):
        peer = lax.rem(me + step, everyone)
        pl.semaphore_signal(
            barrier, inc=1, device_id=(peer // 2, lax.rem(peer, 2)), device_id_type=MESH
        )
        return carry

    lax.fori_loop(1, everyone, greet, 0)
    pl.semaphore_wait(barrier, everyone - 1)


def remote(source, target, sent, landed, device):
    return pltpu.make_async_remote_copy(
        src_ref=source,
        dst_ref=target,
        send_sem=sent,
        recv_sem=landed,
        device_id=device,
        device_id_type=MESH,
    )


def normalize(rows):
    wide = rows.astype(jnp.float32)
    factor = lax.rsqrt(jnp.mean(wide * wide, axis=-1, keepdims=True) + EPS)
    return wide * factor, factor


def lanes(head):
    return pl.ds(pl.multiple_of(head * HD, HD), HD)


def dispatch_kernel(
    heads, q_in, k_in, v_in, c_in, w_ref, ids_ref, full_ref, slots_ref, w_full_ref, x_ref,
    q_ref, k_ref, v_ref, c_ref, loaded, sent, landed, relay_sent, relay_landed, id_sent, id_landed, w_sent, w_landed,
):
    seq_devices = 2 * heads
    chip, core = lax.axis_index("seq"), lax.axis_index("dp")
    other = 1 - core
    seq_here, head_here = chip // heads, lax.rem(chip, heads)
    half = x_ref.shape[2]
    per_core = heads // 2
    pairs = ((q_in, q_ref), (k_in, k_ref), (v_in, v_ref), (c_in, c_ref), (w_ref, w_full_ref.at[core]))
    loads = [
        pltpu.make_async_copy(source, target, loaded.at[i])
        for i, (source, target) in enumerate(pairs)
    ]
    for load in loads:
        load.start()
    greet_all(seq_devices)
    w_copy = remote(w_ref, w_full_ref.at[core], w_sent, w_landed, (chip, other))
    w_copy.start()
    for load in loads:
        load.wait()

    def target(step):
        part = lax.rem(step, 2)
        head = lax.rem(chip + step // 2, heads)
        return part, head, core * heads + head

    def data_copy(step):
        part, head, owner = target(step)
        return remote(
            x_ref.at[head, part],
            full_ref.at[chip, part],
            sent.at[step],
            landed.at[chip],
            (owner, part),
        )

    def id_copy(step):
        part, head, owner = target(step)
        return remote(
            ids_ref, slots_ref.at[chip], id_sent.at[step], id_landed.at[chip], (owner, part)
        )

    def to_self(step):
        part, head, owner = target(step)
        return jnp.logical_and(owner == chip, part == core)

    def send(step):
        part, head, owner = target(step)

        @pl.when(jnp.logical_not(to_self(step)))
        def _():
            id_copy(step).start()
            data_copy(step).start()

        @pl.when(to_self(step))
        def _():
            full_ref[chip, part] = x_ref[head, part]
            slots_ref[chip] = ids_ref[...]

    def fill(head, index, rows):
        for part in range(2):
            x_ref[head, part, :, index * HD : (index + 1) * HD] = rows[
                part * half : (part + 1) * half
            ].astype(x_ref.dtype)

    def prepare(step, carry):
        head = lax.rem(chip + step, heads)
        fill(head, 0, normalize(q_ref[:, lanes(head)])[0])
        fill(head, 1, normalize(k_ref[:, lanes(head)])[0])
        fill(head, 2, v_ref[:, lanes(head)])

        @pl.when(step == 0)
        def _():
            remote(w_ref, w_full_ref.at[other], w_sent, w_landed, (chip, other)).wait_recv()

        w_rows = w_full_ref[head // per_core, lanes(lax.rem(head, per_core)), :]
        grad = lax.dot_general(
            c_ref[...], w_rows, (((1,), (1,)), ((), ())), preferred_element_type=jnp.float32
        )
        fill(head, 3, grad)
        send(2 * step)
        send(2 * step + 1)
        return carry

    lax.fori_loop(0, heads, prepare, 0)

    def relay_copy(source):
        return remote(
            full_ref.at[source, core],
            full_ref.at[source, core],
            relay_sent.at[source],
            relay_landed.at[source],
            (chip, other),
        )

    def receive(step, carry):
        source = lax.rem(head_here - step // 2 + heads, heads) + heads * lax.rem(step, 2)

        @pl.when(jnp.logical_not(jnp.logical_and(source == chip, seq_here == core)))
        def _():
            remote(
                x_ref.at[0, 0],
                full_ref.at[source, core],
                sent.at[0],
                landed.at[source],
                (chip, other),
            ).wait_recv()
            remote(
                ids_ref, slots_ref.at[source], id_sent.at[0], id_landed.at[source], (chip, other)
            ).wait_recv()

        relay_copy(source).start()
        return carry

    lax.fori_loop(0, seq_devices, receive, 0)

    def finish(step, carry):
        remote(
            full_ref.at[step, core],
            full_ref.at[step, other],
            relay_sent.at[step],
            relay_landed.at[step],
            (chip, other),
        ).wait_recv()
        relay_copy(step).wait_send()

        @pl.when(jnp.logical_not(to_self(step)))
        def _():
            id_copy(step).wait_send()
            data_copy(step).wait_send()

        return carry

    lax.fori_loop(0, seq_devices, finish, 0)
    w_copy.wait_send()


def dispatch_call(q, k, v, c, w, ids):
    tokens, features = q.shape
    heads = features // HD
    half, width = tokens // 2, 4 * HD
    n = 2 * heads
    vmem = pl.BlockSpec(memory_space=pltpu.VMEM)
    return pl.pallas_call(
        functools.partial(dispatch_kernel, heads),
        out_shape=(
            jax.ShapeDtypeStruct((n, 2, half, width), q.dtype),
            jax.ShapeDtypeStruct((n,) + ids.shape, ids.dtype),
            jax.ShapeDtypeStruct((2,) + w.shape, w.dtype),
        ),
        in_specs=[pl.BlockSpec(memory_space=pltpu.HBM)] * 5 + [vmem],
        out_specs=(vmem,) * 3,
        scratch_shapes=[pltpu.VMEM((heads, 2, half, width), q.dtype)]
        + [pltpu.VMEM(q.shape, q.dtype)] * 3
        + [pltpu.VMEM(c.shape, c.dtype), pltpu.SemaphoreType.DMA((5,))]
        + [pltpu.SemaphoreType.DMA((n,))] * 6
        + [pltpu.SemaphoreType.DMA] * 2,
        compiler_params=pltpu.CompilerParams(
            collective_id=0, has_side_effects=True, vmem_limit_bytes=40 << 20
        ),
    )(q, k, v, c, w, ids)


def collector(heads, t_ref, mine, out_ref, held, stage, swap_sent, swap_landed, sent, landed):
    seq_devices = 2 * heads
    chip, core = lax.axis_index("seq"), lax.axis_index("dp")
    other = 1 - core
    seq_here, head_here = chip // heads, lax.rem(chip, heads)

    def peer_of(step):
        far = heads * (1 - lax.rem(step, 2))
        return lax.rem(chip + step // 2 + far, seq_devices)

    def swap(peer):
        return remote(
            t_ref.at[other, peer],
            held.at[peer],
            swap_sent.at[peer],
            swap_landed.at[peer],
            (chip, other),
        )

    def send_copy(peer):
        return remote(
            stage.at[peer],
            out_ref.at[head_here, core],
            sent.at[peer],
            landed.at[2 * head_here + core],
            (peer, seq_here),
        )

    def to_self(peer):
        return jnp.logical_and(peer == chip, seq_here == core)

    def begin(step, carry):
        swap(peer_of(step)).start()
        return carry

    def send(step, carry):
        peer = peer_of(step)
        swap(peer).wait_recv()

        @pl.when(jnp.logical_not(to_self(peer)))
        def _():
            stage[peer] = mine(peer) + held[peer]
            send_copy(peer).start()

        @pl.when(to_self(peer))
        def _():
            out_ref[head_here, core] = mine(peer) + held[peer]

        return carry

    def wait_one(step, carry):
        head, part = step // 2, lax.rem(step, 2)
        source = core * heads + head

        @pl.when(jnp.logical_not(jnp.logical_and(source == chip, part == core)))
        def _():
            remote(
                stage.at[0], out_ref.at[head, part], sent.at[0], landed.at[step], (chip, other)
            ).wait_recv()

        swap(step).wait_send()

        @pl.when(jnp.logical_not(to_self(step)))
        def _():
            send_copy(step).wait_send()

        return carry

    return (
        lambda: lax.fori_loop(0, seq_devices, begin, 0),
        lambda low, high: lax.fori_loop(low, high, send, 0),
        wait_one,
    )


def final_kernel(
    heads, scale, t_ref, t_attn, q_ref, k_ref, c_ref, proj_ref,
    gq_ref, gk_ref, gv_ref, out_ref, grad_ref,
    own, own_loaded, got, held, stage, got_attn, held_attn, stage_attn, a_ref, w_ref, w_held, kept, x_stage, x_got, y_stage, y_got, z_stage, z_got,
    swap_sent, swap_landed, sent, landed, w_swap_sent, w_swap_landed,
    attn_swap_sent, attn_swap_landed, attn_sent, attn_landed,
    x_sent, x_landed, y_sent, y_landed, z_sent, z_landed,
):
    seq_devices = 2 * heads
    quarter = seq_devices // 4
    chip, core = lax.axis_index("seq"), lax.axis_index("dp")
    other = 1 - core
    x, y, z = lax.rem(chip, 2), lax.rem(chip // 2, 2), chip // 4
    half = got.shape[2]
    start_swaps, send_all, wait_one = collector(
        heads, t_ref, lambda peer: own[peer], got, held, stage, swap_sent, swap_landed, sent, landed
    )
    start_attn, send_attn, wait_attn = collector(
        heads, t_attn, lambda peer: t_attn[core, peer], got_attn, held_attn, stage_attn,
        attn_swap_sent, attn_swap_landed, attn_sent, attn_landed,
    )
    load = pltpu.make_async_copy(t_ref.at[core], own, own_loaded)
    load.start()
    greet_all(seq_devices)

    def w_swap(peer):
        return remote(
            w_ref.at[peer, other],
            w_held.at[peer],
            w_swap_sent.at[peer],
            w_swap_landed.at[peer],
            (chip, other),
        )

    def x_copy(j):
        return remote(
            x_stage.at[j], x_got.at[j], x_sent.at[j], x_landed.at[j], (chip + 1 - 2 * x, core)
        )

    def y_copy(j):
        return remote(
            y_stage.at[j], y_got.at[j], y_sent.at[j], y_landed.at[j], (chip + 2 - 4 * y, core)
        )

    def z_copy(j):
        return remote(
            z_stage.at[j], z_got.at[z], z_sent.at[j], z_landed.at[z], (4 * j + 2 * y + x, core)
        )

    def both_cores(peer):
        w_swap(peer).wait_recv()
        return w_ref[peer, core].astype(jnp.float32) + w_held[peer].astype(jnp.float32)

    piece = w_ref.shape[2]

    def term(head, carry):
        total = None
        for part in range(2):
            wait_attn(2 * head + part, 0)
            rows = slice(part * half, (part + 1) * half)
            block = got_attn[head, part]
            a_ref[rows, lanes(head)] = block
            partial = lax.dot_general(
                block, c_ref[rows, :], (((0,), (0,)), ((), ())), preferred_element_type=jnp.float32
            )
            total = partial if total is None else total + partial
        for index in range(4):
            w_ref[2 * head + index // 2, index % 2] = total[
                index * piece : (index + 1) * piece
            ].astype(w_ref.dtype)
        w_swap(2 * head).start()
        w_swap(2 * head + 1).start()
        return carry

    def x_phase(j, carry):
        x_stage[j] = both_cores(2 * j + 1 - x).astype(x_stage.dtype)
        x_copy(j).start()
        kept[j] = both_cores(2 * j + x)
        return carry

    def y_phase(j, carry):
        away, here = 2 * j + 1 - y, 2 * j + y
        x_copy(away).wait_recv()
        y_stage[j] = (kept[away] + x_got[away].astype(jnp.float32)).astype(y_stage.dtype)
        y_copy(j).start()
        x_copy(here).wait_recv()
        kept[here] += x_got[here].astype(jnp.float32)
        return carry

    def z_phase(j, carry):
        y_copy(j).wait_recv()
        total = kept[2 * j + y] + y_got[j].astype(jnp.float32)

        @pl.when(j != z)
        def _():
            z_stage[j] = total.astype(z_stage.dtype)
            z_copy(j).start()

        @pl.when(j == z)
        def _():
            grad_ref[...] = total

        return carry

    def z_sum(j, carry):
        @pl.when(j != z)
        def _():
            remote(
                z_stage.at[j], z_got.at[j], z_sent.at[j], z_landed.at[j], (4 * j + 2 * y + x, core)
            ).wait_recv()
            grad_ref[...] += z_got[j].astype(jnp.float32)
            z_copy(j).wait_send()

        y_copy(j).wait_send()
        return carry

    def ends(j, carry):
        x_copy(j).wait_send()
        w_swap(2 * j).wait_send()
        w_swap(2 * j + 1).wait_send()
        return carry

    start_attn()
    start_swaps()
    send_attn(0, seq_devices)
    load.wait()
    send_all(0, heads)
    lax.fori_loop(0, heads, term, 0)
    lax.fori_loop(0, seq_devices // 2, x_phase, 0)
    send_all(heads, seq_devices)
    lax.fori_loop(0, quarter, y_phase, 0)
    lax.fori_loop(0, quarter, z_phase, 0)

    depth = proj_ref.shape[1]
    tile = 2 * HD

    def project(step, carry):
        columns = pl.ds(pl.multiple_of(step * tile, tile), tile)
        total = jnp.dot(
            a_ref[:, :depth], proj_ref[0, :, columns], preferred_element_type=jnp.float32
        ) + jnp.dot(a_ref[:, depth:], proj_ref[1, :, columns], preferred_element_type=jnp.float32)
        out_ref[:, columns] = total.astype(out_ref.dtype)
        return carry

    lax.fori_loop(0, out_ref.shape[1] // tile, project, 0)

    def finish(step, carry):
        wait_one(step, carry)
        head, part = step // 2, lax.rem(step, 2)
        rows = pl.ds(pl.multiple_of(part * half, half), half)
        for index, (source, target) in enumerate(((q_ref, gq_ref), (k_ref, gk_ref))):
            normed, factor = normalize(source[rows, lanes(head)])
            gradient = got[head, part, :, index * HD : (index + 1) * HD].astype(jnp.float32)
            inner = jnp.mean(gradient * normed, axis=-1, keepdims=True)
            target[rows, lanes(head)] = (factor * (gradient - normed * inner)).astype(target.dtype)
        gv_ref[rows, lanes(head)] = got[head, part, :, 2 * HD :]
        return carry

    lax.fori_loop(0, seq_devices, finish, 0)
    lax.fori_loop(0, quarter, z_sum, 0)
    grad_ref[...] = grad_ref[...] * scale
    lax.fori_loop(0, seq_devices // 2, ends, 0)


def final_call(heads, scale, rows, attn_rows, q, k, cotan, w_full):
    _, n, half, width = rows.shape
    vmem = pl.BlockSpec(memory_space=pltpu.VMEM)
    piece = (q.shape[1] // (2 * n), w_full.shape[2])
    kind = rows.dtype
    args = (rows, attn_rows, q, k, cotan, w_full)
    like = jax.ShapeDtypeStruct(q.shape, kind)
    projected = jax.ShapeDtypeStruct((q.shape[0], w_full.shape[2]), kind)
    counts = [n] * 10 + [n // 2] * 2 + [n // 4] * 4
    return pl.pallas_call(
        functools.partial(final_kernel, heads, scale),
        out_shape=(like, like, like, projected, jax.ShapeDtypeStruct(piece, jnp.float32)),
        in_specs=[pl.BlockSpec(memory_space=pl.ANY)] + [vmem] * 5,
        out_specs=(vmem,) * 5,
        scratch_shapes=[
            pltpu.VMEM((n, half, width), kind),
            pltpu.SemaphoreType.DMA,
            pltpu.VMEM((heads, 2, half, width), kind),
            pltpu.VMEM((n, half, width), kind),
            pltpu.VMEM((n, half, width), kind),
            pltpu.VMEM((heads, 2, half, HD), kind),
            pltpu.VMEM((n, half, HD), kind),
            pltpu.VMEM((n, half, HD), kind),
            pltpu.VMEM(q.shape, kind),
            pltpu.VMEM((n, 2) + piece, kind),
            pltpu.VMEM((n,) + piece, kind),
            pltpu.VMEM((n // 2,) + piece, jnp.float32),
            pltpu.VMEM((n // 2,) + piece, kind),
            pltpu.VMEM((n // 2,) + piece, kind),
        ]
        + [pltpu.VMEM((n // 4,) + piece, kind)] * 4
        + [pltpu.SemaphoreType.DMA((count,)) for count in counts],
        compiler_params=pltpu.CompilerParams(
            collective_id=2, has_side_effects=True, vmem_limit_bytes=48 << 20
        ),
    )(*args)


def per_device_heads(queries, key_rows, value_rows, cotangent, w_out, cluster_ids):
    tokens, features = queries.shape[1], queries.shape[2]
    heads = features // HD
    seq_devices = lax.axis_size("seq")
    half = tokens // 2
    clusters = CL_DEV * seq_devices
    capacity = 2 * tokens // clusters
    core = lax.axis_index("dp")
    labels = cluster_ids[0]
    positions = jnp.arange(tokens)
    matching = labels[:, None] == labels[None, :]
    earlier = positions[None, :] < positions[:, None]
    ranks = jnp.sum(jnp.logical_and(matching, earlier), axis=1)
    slot_index = (labels * capacity + ranks).astype(jnp.int32)
    ids = slot_index.reshape(2, half)

    cotan = cotangent[0]
    width = 4 * HD
    full, landed_ids, w_full = dispatch_call(
        queries[0], key_rows[0], value_rows[0], cotan, w_out, ids
    )
    slots = landed_ids.reshape(seq_devices, tokens)
    my_slots = clusters * capacity // 2
    wanted = core * my_slots + jnp.arange(my_slots)
    one_hot = (slots[:, None, :] == wanted[None, :, None]).astype(jnp.bfloat16)
    packed = jnp.einsum(
        "dst,dtf->dsf",
        one_hot,
        full.reshape(seq_devices, tokens, width),
        preferred_element_type=jnp.float32,
    ).astype(jnp.bfloat16)
    packed = packed.reshape(seq_devices, clusters // 2, capacity, width)
    packed = jnp.transpose(packed, (1, 0, 2, 3))
    packed = packed.reshape(clusters // 2, seq_devices * capacity, width)
    q_blk, k_blk, v_blk, d_blk = [packed[:, :, i * HD : (i + 1) * HD] for i in range(4)]
    taken = jnp.sum(one_hot.astype(jnp.float32), axis=2)
    taken = taken.reshape(seq_devices, clusters // 2, capacity)
    key_valid = jnp.transpose(taken, (1, 0, 2)).reshape(clusters // 2, -1) > 0

    def take(blocks):
        count = len(blocks)
        joined = jnp.concatenate(blocks, axis=-1)
        joined = joined.reshape(clusters // 2, seq_devices, capacity, count * HD)
        joined = jnp.transpose(joined, (1, 0, 2, 3)).reshape(seq_devices, my_slots, count * HD)
        rows = jnp.einsum(
            "dspt,dsf->pdtf",
            one_hot.reshape(seq_devices, my_slots, 2, half),
            joined,
            preferred_element_type=jnp.float32,
        )
        return rows.astype(jnp.bfloat16)

    attn_blk, probs, probs_b = attend(q_blk, k_blk, v_blk, key_valid)
    grads = attend_back(q_blk, k_blk, v_blk, probs, probs_b, attn_blk, d_blk)
    scale = 1.0 / math.sqrt(tokens * seq_devices * 2)
    grad_queries, grad_keys, grad_values, projected, weight_grad = final_call(
        heads, scale, take(list(grads)), take([attn_blk]), queries[0], key_rows[0], cotan, w_full
    )
    return (projected[None], grad_queries[None], grad_keys[None], grad_values[None], weight_grad)


def per_device(queries, *rest):
    heads = queries.shape[2] // HD
    if lax.axis_size("dp") == 2 and lax.axis_size("seq") == 2 * heads:
        return per_device_heads(queries, *rest)
    return per_device_slots(queries, *rest)


def solution(mesh):
    in_specs = (
        P("dp", "seq", None),
        P("dp", "seq", None),
        P("dp", "seq", None),
        P("dp", "seq", None),
        P("dp", None),
        P("dp", "seq"),
    )
    out_specs = (
        P("dp", "seq", None),
        P("dp", "seq", None),
        P("dp", "seq", None),
        P("dp", "seq", None),
        P(("seq", "dp"), None),
    )
    return jax.shard_map(
        per_device, mesh=mesh, in_specs=in_specs, out_specs=out_specs, check_vma=False
    )
```

profile of v0, /device:TPU:0, one launch (start us, length us, event | category | flops | bytes accessed | tf_op | source)
XLA Modules:
  0.0 147.6 jit_solution(881260044861330042)
XLA Ops:
  0.6 0.9 convert_reduce_fusion.1
  1.6 0.7 broadcast_multiply_fusion
  2.3 0.0 copy-start.1
  2.3 1.0 copy-done.1
  3.3 1.0 copy-done.3
  4.4 1.0 copy-done.5
  5.4 1.2 copy-done.7
  6.7 1.0 copy-done.8
  7.7 59.2 %shard_map.101 = (bf16[16,2,128,512]{3,2,1,0:T(8,128)(2,1)S(1)}, s32[16,2,128]{2,1,0:T(2,128)S(1)}, bf16[2,512,1024]{2,1,0:T(8,128)(2,1)S(1)}) custom-call(bf16[256,1024]{1,0:T(8,128)(2,1)S(1)} %bitcast.82, bf16[256,1024]{1,0:T(8,128)(2,1)S(1)} %bitcast.84, bf16[256,1024]{1,0:T(8,128)(2,1)S(1)} %bitcast.92, bf16[256,1024]{1,0:T(8,128)(2,1)S(1)} %bitcast.86, ...), custom_call_target="tpu_custom_call" | custom-call | tf_op jit(solution)/shard_map/pallas_call | solution.py:337
  67.0 1.3 convert_bitcast_fusion
  68.3 0.7 convert_reduce_fusion
  69.0 2.5 %copy.97 = bf16[32,16,8,512]{3,2,1,0:T(8,128)(2,1)} copy(bf16[32,16,8,512]{3,2,0,1:T(8,128)(2,1)S(1)} %convert_bitcast_fusion) | data formatting | bytes 8388608 | tf_op jit(solution)/shard_map/transpose | solution.py:666
  71.5 0.1 copy.49
  71.6 0.1 copy.50
  71.7 0.1 copy.51
  71.8 3.3 %fusion.29 = f32[32,128,128]{1,2,0:T(8,128)S(1)} fusion(pred[128,128]{0,1:T(8,128)(4,1)S(1)} %get-tuple-element.23, pred[128,128]{0,1:T(8,128)(4,1)S(1)} %get-tuple-element.24, pred[32,128]{1,0:T(8,128)(4,1)S(1)} %copy.51, bf16[32,128,512]{2,1,0:T(8,128)(2,1)} %bitcast.94), kind=kOutput, calls=%fused_computation.33 | convolution fusion | flops 136843392 | bytes 4231168 | tf_op jit(solution)/shard_map/div | solution.py:48
  75.1 1.8 %fusion.20 = bf16[32,16,8,128]{3,2,1,0:T(8,128)(2,1)S(1)} fusion(bf16[32,128,512]{2,1,0:T(8,128)(2,1)} %bitcast.95, f32[32,128,128]{1,2,0:T(8,128)S(1)} %fusion.29), kind=kOutput, calls=%fused_computation.26 | convolution fusion | flops 135266304 | bytes 4194304 | tf_op jit(solution)/shard_map/chqk,cqhd->ckhd/dot_general | solution.py:59
  76.9 0.7 copy-done.9
  77.6 1.0 fusion.14
  78.6 0.9 multiply_convert_fusion.2
  79.5 0.4 fusion.25
  80.0 0.5 fusion.24
  80.5 2.9 %convert_bitcast_fusion.1.t_ref = bf16[2,16,128,384]{3,2,1,0:T(8,128)(2,1)} fusion(s32[16,2,128]{2,1,0:T(2,128)S(1)} %get-tuple-element.13, s32[256]{0:T(256)S(1)} %iota_add_fusion, bf16[32,16,8,128]{3,2,1,0:T(8,128)(2,1)S(1)} %fusion.20, bf16[32,16,8,128]{3,2,1,0:T(8,128)(2,1)S(1)} %fusion.25, bf16[32,16,8,128]{3,2,1,0:T(8,128)(2,1)S(1)} %fusion.24), kind=kOutput, calls=%fused_computation.13 | convolution fusion | flops 817364992 | bytes 6308864 | tf_op jit(solution)/shard_map/dspt,dsf->pdtf/dot_general | solution.py:678
  83.4 1.4 fusion.21.t_attn
  84.8 0.0 copy-done.2
  84.8 0.0 copy-done.4
  84.8 59.0 %shard_map.102 = (bf16[256,1024]{1,0:T(8,128)(2,1)S(1)}, bf16[256,1024]{1,0:T(8,128)(2,1)S(1)}, bf16[256,1024]{1,0:T(8,128)(2,1)S(1)}, bf16[256,1024]{1,0:T(8,128)(2,1)S(1)}, f32[32,1024]{1,0:T(8,128)S(1)}) custom-call(bf16[2,16,128,384]{3,2,1,0:T(8,128)(2,1)} %convert_bitcast_fusion.1.t_ref, bf16[2,16,128,128]{3,2,1,0:T(8,128)(2,1)S(1)} %fusion.21.t_attn, ...), custom_call_target="tpu_custom_call" | custom-call | tf_op jit(solution)/shard_map/pallas_call | solution.py:605
  143.8 0.8 copy.104
  144.6 0.8 copy.105
  145.3 0.8 copy.106
  146.1 0.8 copy.107
  146.9 0.7 copy.108
  (16 shorter events, 0.1 us)
Async XLA Ops:
  2.3 1.0 copy-start.1
  3.3 1.0 copy-start.3
  4.4 1.0 copy-start.5
  5.4 1.2 copy-start.7
  6.7 1.0 copy-start.8
  66.9 1.3 copy-start
  75.1 2.5 %copy-start.9 = (bf16[32,16,8,512]{3,2,1,0:T(8,128)(2,1)S(1)}, bf16[32,16,8,512]{3,2,1,0:T(8,128)(2,1)}, u32[]{:S(2)}) copy-start(bf16[32,16,8,512]{3,2,1,0:T(8,128)(2,1)} %copy.97) | copy-start | bytes 12582916
  83.4 1.4 copy-start.2
  83.4 1.4 copy-start.4
  83.4 1.4 copy-start.6
where the time goes:
time: 149 us; the launch traced here: 148 us
  Pallas kernels  118 us (79%)
  matrix products  13.5 us (9%)
  local copies, waits for them, and re-layouts  12.8 us (9%)
  other arithmetic  2.36 us (2%)
    pallas_call x1, Pallas kernels, dispatch_call(): pl.pallas_call(functools.partial(dispatch_kernel, heads), out_shape=(jax....  59.2 us
    pallas_call x1, Pallas kernels, final_call(): pl.pallas_call(functools.partial(final_kernel, heads, scale), out_shape=(...  59 us
    unnamed x26, local copies, waits for them, and re-layouts  9.93 us
    dot_general x2, matrix products, take(): jnp.einsum('dspt,dsf->pdtf', one_hot.reshape(seq_devices, my_slots, 2, ha...  4.24 us
    div x1, matrix products, attend(): probs = weights / jnp.sum(weights, axis=-1, keepdims=True)  3.27 us

commit v1 on v0

v1 whole, which is shorter than its diff:
```python
import functools
import math

import jax
import jax.numpy as jnp
from jax import lax
from jax.experimental import pallas as pl
from jax.experimental.pallas import tpu as pltpu
from jax.sharding import PartitionSpec as P

MESH = pl.DeviceIdType.MESH
HD = 128
CL_DEV = 4


EPS = 1e-06


def head_norm(matrix):
    shaped = matrix.astype(jnp.float32).reshape(matrix.shape[0], matrix.shape[1] // HD, HD)
    factor = lax.rsqrt(jnp.mean(shaped * shaped, axis=-1, keepdims=True) + EPS)
    return (shaped * factor, factor)


def norm_back(gradient, normed, factor):
    shaped = gradient.astype(jnp.float32).reshape(normed.shape)
    inner = jnp.mean(shaped * normed, axis=-1, keepdims=True)
    return (factor * (shaped - normed * inner)).reshape(normed.shape[0], -1)


def split_heads(blocks):
    return blocks.reshape(blocks.shape[0], blocks.shape[1], blocks.shape[2] // HD, HD)


def attend(q_blk, k_blk, v_blk, key_valid):
    q_four, k_four, v_four = (split_heads(q_blk), split_heads(k_blk), split_heads(v_blk))
    scores = jnp.einsum(
        "cqhd,ckhd->chqk", q_four, k_four, preferred_element_type=jnp.float32
    ) / math.sqrt(HD)
    positions = jnp.arange(q_blk.shape[1])
    below_diag = positions[None, :] <= positions[:, None]
    on_diagonal = positions[None, :] == positions[:, None]
    allowed = jnp.logical_or(
        jnp.logical_and(key_valid[:, None, None, :], below_diag[None, None]),
        on_diagonal[None, None],
    )
    weights = jnp.where(allowed, jnp.exp(scores), 0.0)
    probs = weights / jnp.sum(weights, axis=-1, keepdims=True)
    probs_b = probs.astype(jnp.bfloat16)
    attn = jnp.einsum(
        "chqk,ckhd->cqhd", probs_b, v_four, preferred_element_type=jnp.float32
    ).astype(jnp.bfloat16)
    return (attn.reshape(q_blk.shape), probs, probs_b)


def attend_back(q_blk, k_blk, v_blk, probs, probs_b, attn, d_blk):
    q_four, k_four, v_four = (split_heads(q_blk), split_heads(k_blk), split_heads(v_blk))
    d_four, a_four = (split_heads(d_blk), split_heads(attn))
    grad_value = jnp.einsum(
        "chqk,cqhd->ckhd", probs_b, d_four, preferred_element_type=jnp.float32
    ).astype(jnp.bfloat16)
    grad_prob = jnp.einsum("cqhd,ckhd->chqk", d_four, v_four, preferred_element_type=jnp.float32)
    delta_row = jnp.sum(d_four.astype(jnp.float32) * a_four.astype(jnp.float32), axis=-1)
    grad_score = (probs * (grad_prob - jnp.transpose(delta_row, (0, 2, 1))[..., None])).astype(
        jnp.bfloat16
    )
    grad_qhat = jnp.einsum(
        "chqk,ckhd->cqhd", grad_score, k_four, preferred_element_type=jnp.float32
    ) / math.sqrt(HD)
    grad_khat = jnp.einsum(
        "chqk,cqhd->ckhd", grad_score, q_four, preferred_element_type=jnp.float32
    ) / math.sqrt(HD)
    shape = q_blk.shape
    return (
        grad_qhat.astype(jnp.bfloat16).reshape(shape),
        grad_khat.astype(jnp.bfloat16).reshape(shape),
        grad_value.reshape(shape),
    )


def per_device_slots(queries, key_rows, value_rows, cotangent, w_out, cluster_ids):
    token_count = queries.shape[1]
    features = queries.shape[2]
    seq_devices = lax.axis_size("seq")
    data_devices = lax.axis_size("dp")
    capacity = 2 * token_count // (CL_DEV * seq_devices)
    total_slots = 2 * token_count
    labels = cluster_ids[0]
    positions = jnp.arange(token_count)
    matching = labels[:, None] == labels[None, :]
    earlier = positions[None, :] < positions[:, None]
    ranks = jnp.sum(jnp.logical_and(matching, earlier), axis=1)
    slot_index = labels * capacity + ranks

    def pack(matrix):
        empty = jnp.zeros((total_slots, matrix.shape[1]), matrix.dtype)
        return (
            empty.at[slot_index].set(matrix).reshape(seq_devices, CL_DEV, capacity, matrix.shape[1])
        )

    def unpack(returned):
        return returned.reshape(total_slots, -1)[slot_index]

    taken_slots = (
        jnp.zeros((total_slots,), jnp.bfloat16)
        .at[slot_index]
        .set(1.0)
        .reshape(seq_devices, CL_DEV, capacity)
    )
    q_norm, q_factor = head_norm(queries[0])
    k_norm, k_factor = head_norm(key_rows[0])
    q_hat = q_norm.reshape(token_count, features).astype(jnp.bfloat16)
    k_hat = k_norm.reshape(token_count, features).astype(jnp.bfloat16)
    cotan = cotangent[0]
    w_full = lax.all_gather(w_out, "dp", axis=0, tiled=True)
    received = (
        lax.all_to_all(pack(q_hat), "seq", split_axis=0, concat_axis=2, tiled=True),
        lax.all_to_all(pack(k_hat), "seq", split_axis=0, concat_axis=2, tiled=True),
        lax.all_to_all(pack(value_rows[0]), "seq", split_axis=0, concat_axis=2, tiled=True),
        lax.all_to_all(taken_slots, "seq", split_axis=0, concat_axis=2, tiled=True),
    )
    q_blk, k_blk, v_blk = (received[0][0], received[1][0], received[2][0])
    key_valid = received[3][0] > 0
    attn_blk, probs, probs_b = attend(q_blk, k_blk, v_blk, key_valid)
    attn_back = lax.all_to_all(attn_blk[None], "seq", split_axis=2, concat_axis=0, tiled=True)
    attn = unpack(attn_back)
    grad_attn = lax.dot_general(
        cotan, w_full, (((1,), (1,)), ((), ())), preferred_element_type=jnp.float32
    ).astype(jnp.bfloat16)
    grad_recv = lax.all_to_all(pack(grad_attn), "seq", split_axis=0, concat_axis=2, tiled=True)
    grad_qblk, grad_kblk, grad_vblk = attend_back(
        q_blk, k_blk, v_blk, probs, probs_b, attn_blk, grad_recv[0]
    )
    grads_back = (
        lax.all_to_all(grad_qblk[None], "seq", split_axis=2, concat_axis=0, tiled=True),
        lax.all_to_all(grad_kblk[None], "seq", split_axis=2, concat_axis=0, tiled=True),
        lax.all_to_all(grad_vblk[None], "seq", split_axis=2, concat_axis=0, tiled=True),
    )
    grad_qhat, grad_khat, grad_values = (
        unpack(grads_back[0]),
        unpack(grads_back[1]),
        unpack(grads_back[2]),
    )
    projected = jnp.dot(attn, w_full, preferred_element_type=jnp.float32).astype(jnp.bfloat16)
    grad_queries = norm_back(grad_qhat, q_norm, q_factor).astype(jnp.bfloat16)
    grad_keys = norm_back(grad_khat, k_norm, k_factor).astype(jnp.bfloat16)
    local_term = lax.dot_general(
        attn, cotan, (((0,), (0,)), ((), ())), preferred_element_type=jnp.float32
    )
    summed = lax.psum_scatter(local_term, ("seq", "dp"), scatter_dimension=0, tiled=True)
    weight_grad = summed / math.sqrt(token_count * seq_devices * data_devices)
    return (projected[None], grad_queries[None], grad_keys[None], grad_values[None], weight_grad)


def remote(source, target, sent, landed, device):
    return pltpu.make_async_remote_copy(
        src_ref=source,
        dst_ref=target,
        send_sem=sent,
        recv_sem=landed,
        device_id=device,
        device_id_type=MESH,
    )


def normalize(rows):
    wide = rows.astype(jnp.float32)
    factor = lax.rsqrt(jnp.mean(wide * wide, axis=-1, keepdims=True) + EPS)
    return wide * factor, factor


def lanes(head):
    return pl.ds(pl.multiple_of(head * HD, HD), HD)


def dot(a, b, ca, cb):
    return lax.dot_general(a, b, (((ca,), (cb,)), ((), ())), preferred_element_type=jnp.float32)


def layer_kernel(
    heads, scale,
    q_in, k_in, v_in, c_in, w_in, labels_ref,
    gq_ref, gk_ref, gv_ref, out_ref, grad_ref,
    q_ref, k_ref, v_ref, c_ref, w_full, x_ref, full, xfull, ids_ref, slots,
    onehot_t, qk, gv, e_ref, num, den, own_out, cross_out, st_mine, st_got,
    stage_a, stage_g, stage_x, got_a, got_g, got_x,
    a_ref, w_ref, w_held, kept, x_stage, x_got, y_stage, y_got, z_stage, z_got,
    loaded, w_sent, w_landed, sent, landed, xsent, xlanded, id_sent, id_landed, st_sent, st_landed,
    a_sent, a_landed, g_sent, g_landed, cx_sent, cx_landed,
    w_swap_sent, w_swap_landed, x_sent, x_landed, y_sent, y_landed, z_sent, z_landed,
):
    n = 2 * heads
    quarter = n // 4
    pairs = heads // 2
    chip, core = lax.axis_index("seq"), lax.axis_index("dp")
    other = 1 - core
    side, here = chip // heads, lax.rem(chip, heads)
    base, far = side * heads, (1 - side) * heads
    x, y, z = lax.rem(chip, 2), lax.rem(chip // 2, 2), chip // 4
    heavy = side == core
    light = jnp.logical_not(heavy)
    first = core == 0
    tokens = q_ref.shape[0]
    kind = q_ref.dtype
    clusters = qk.shape[1]
    rows_of = qk.shape[2]
    blocks = clusters // 2
    cap = rows_of // heads
    nslots = clusters * cap
    inv = 1.0 / math.sqrt(HD)

    ins = ((q_in, q_ref), (k_in, k_ref), (v_in, v_ref), (c_in, c_ref), (w_in, w_full.at[core]))
    loads = [
        pltpu.make_async_copy(source, target, loaded.at[i])
        for i, (source, target) in enumerate(ins)
    ]
    for load in loads:
        load.start()

    barrier = pltpu.get_barrier_semaphore()

    def greet(step, carry):
        pl.semaphore_signal(
            barrier, inc=1, device_id=(lax.rem(chip + step, n), core), device_id_type=MESH
        )
        return carry

    lax.fori_loop(1, n, greet, 0)
    pl.semaphore_signal(barrier, inc=1, device_id=(chip, other), device_id_type=MESH)

    wide = jnp.broadcast_to(labels_ref[...].astype(jnp.float32), (tokens, tokens))
    before = lax.broadcasted_iota(jnp.int32, wide.shape, 0) < lax.broadcasted_iota(
        jnp.int32, wide.shape, 1
    )
    same = jnp.logical_and(wide.T == wide, before)
    rank = jnp.sum(jnp.where(same, 1.0, 0.0), axis=0, keepdims=True)
    ids_ref[...] = jnp.broadcast_to(wide[0:1] * cap + rank, ids_ref.shape)
    slots[chip] = ids_ref[...]

    pl.semaphore_wait(barrier, n)
    w_copy = remote(w_in, w_full.at[core], w_sent, w_landed, (chip, other))
    w_copy.start()

    def data_copy(head):
        return remote(
            x_ref.at[head], full.at[here], sent.at[head], landed.at[here], (base + head, core)
        )

    def cross_copy(head):
        lane = pl.ds(pl.multiple_of(core * 2 * HD, 2 * HD), 2 * HD)
        return remote(
            x_ref.at[head, :, lane], xfull.at[here], xsent.at[head], xlanded.at[here],
            (far + head, core),
        )

    def id_copy(peer):
        return remote(ids_ref, slots.at[chip], id_sent.at[peer], id_landed.at[chip], (peer, core))

    def send_ids(step, carry):
        head = lax.rem(here + step, heads)

        @pl.when(step > 0)
        def _():
            id_copy(base + head).start()

        @pl.when(light)
        def _():
            id_copy(far + head).start()

        return carry

    lax.fori_loop(0, heads, send_ids, 0)
    for load in loads:
        load.wait()

    per_core = heads // 2

    def prepare(step, carry):
        head = lax.rem(here + step + 1, heads)
        x_ref[head, :, 0:HD] = normalize(q_ref[:, lanes(head)])[0].astype(kind)
        x_ref[head, :, 2 * HD : 3 * HD] = normalize(k_ref[:, lanes(head)])[0].astype(kind)
        x_ref[head, :, 3 * HD : 4 * HD] = v_ref[:, lanes(head)]

        @pl.when(step == 0)
        def _():
            remote(w_in, w_full.at[other], w_sent, w_landed, (chip, other)).wait_recv()

        w_rows = w_full[head // per_core, lanes(lax.rem(head, per_core)), :]
        x_ref[head, :, HD : 2 * HD] = dot(c_ref[...], w_rows, 1, 1).astype(kind)

        @pl.when(light)
        def _():
            cross_copy(head).start()

        @pl.when(step < heads - 1)
        def _():
            data_copy(head).start()

        @pl.when(step == heads - 1)
        def _():
            full[here] = x_ref[here]

        return carry

    lax.fori_loop(0, heads, prepare, 0)

    def wait_ids(peer):
        remote(ids_ref, slots.at[peer], id_sent.at[0], id_landed.at[peer], (chip, other)).wait_recv()

    def pack_one(peer, rows):
        slot_row = slots[peer]
        down = lax.broadcasted_iota(jnp.int32, (nslots, tokens), 0).astype(jnp.float32)
        hot = jnp.where(down == slot_row[0:1], 1.0, 0.0)
        along = lax.broadcasted_iota(jnp.int32, (tokens, nslots), 1).astype(jnp.float32)
        onehot_t[peer] = jnp.where(along == slot_row.T[:, 0:1], 1.0, 0.0).astype(kind)
        valid = jnp.broadcast_to(jnp.sum(hot, axis=1, keepdims=True), (nslots, HD))
        packed = dot(hot.astype(kind), rows, 1, 0)
        packed = packed.reshape(clusters, cap, packed.shape[1])
        return packed, valid.reshape(clusters, cap, HD)

    def pair_rows(pair):
        return pl.ds(pl.multiple_of(pair * 2 * cap, 2 * cap), 2 * cap)

    def pack_own(step, carry):
        pair = lax.rem(here // 2 + pairs - step, pairs)
        parts, valids = [], []
        for index in range(2):
            source = 2 * pair + index

            @pl.when(source != here)
            def _():
                wait_ids(base + source)
                remote(
                    x_ref.at[0], full.at[source], sent.at[0], landed.at[source], (chip, other)
                ).wait_recv()

            packed, valid = pack_one(base + source, full[source])
            parts.append(packed)
            valids.append(valid)
        both = jnp.concatenate(parts, axis=1).astype(kind)
        rows = pair_rows(pair)
        qk[0, :, rows, :] = both[:, :, 0:HD]
        gv[0, :, rows, 0:HD] = both[:, :, HD : 2 * HD]
        qk[1, :, rows, :] = both[:, :, 2 * HD : 3 * HD]
        gv[1, :, rows, 0:HD] = both[:, :, 3 * HD :]
        gv[1, :, rows, HD:] = jnp.concatenate(valids, axis=1).astype(kind)
        return carry

    def pack_cross(step, carry):
        pair = lax.rem(here // 2 + pairs - step, pairs)
        parts, valids = [], []
        for index in range(2):
            source = 2 * pair + index
            wait_ids(far + source)
            remote(
                x_ref.at[0, :, 0 : 2 * HD], xfull.at[source], xsent.at[0], xlanded.at[source],
                (chip, other),
            ).wait_recv()
            packed, valid = pack_one(far + source, xfull[source])
            parts.append(packed)
            valids.append(valid)
        both = jnp.concatenate(parts, axis=1).astype(kind)
        rows = pair_rows(pair)
        qk[2, :, rows, :] = both[:, :, 0:HD]
        gv[2, :, rows, 0:HD] = both[:, :, HD:]
        gv[2, :, rows, HD:] = jnp.concatenate(valids, axis=1).astype(kind)
        return carry

    size = 2 * rows_of
    down = lax.broadcasted_iota(jnp.int32, (size, size), 0)
    along = lax.broadcasted_iota(jnp.int32, (size, size), 1)
    lane = lax.broadcasted_iota(jnp.int32, (size, HD), 1)
    group = 2

    def one_cluster():
        return down // rows_of == along // rows_of

    def of(ref, index, block, low, high):
        part = ref[index, pl.ds(2 * block, 2), :, low:high]
        return part.reshape(size, high - low)

    def put(ref, block, low, value):
        width = value.shape[1]
        ref[pl.ds(2 * block, 2), :, low : low + width] = value.astype(kind).reshape(
            2, rows_of, width
        )

    def forward(block, qi, ki, vi, allowed):
        scores = dot(of(qk, qi, block, 0, HD), of(qk, ki, block, 0, HD), 1, 1)
        weights = jnp.where(allowed, jnp.exp(scores * inv), 0.0).astype(kind)
        both = dot(weights, of(gv, vi, block, 0, 2 * HD), 1, 0)
        return weights, both[:, :HD], both[:, HD:]

    def diagonal(step, carry):
        allowed = jnp.logical_and(one_cluster(), along <= down)
        found = [forward(step * group + i, 0, 1, 1, allowed) for i in range(group)]
        for i, (weights, top, total) in enumerate(found):
            e_ref[0, step * group + i] = weights
            num[0, step * group + i] = top
            den[0, step * group + i] = total
        return carry

    cross_rows = other
    cross_q, cross_k = 2 * other, 1 + core
    cross_g, cross_v = 2 * other, 1 + core

    def across(step, carry):
        found = []
        for i in range(group):
            block = step * group + i
            weights, top, total = forward(block, cross_q, cross_k, cross_v, one_cluster())
            share = core.astype(jnp.float32)
            found.append((weights, top + num[0, block] * share, total + den[0, block] * share))
        for i, (weights, top, total) in enumerate(found):
            e_ref[1, step * group + i] = weights
            num[cross_rows, step * group + i] = top
            den[cross_rows, step * group + i] = total
        return carry

    def inner(block, rows, grads):
        return jnp.sum(
            of(gv, grads, block, 0, HD).astype(jnp.float32) * num[rows, block],
            axis=1, keepdims=True,
        )

    def settle(block, rows, total, top):
        factor = 1.0 / jnp.where(total > 0, total, 1.0)
        attn = num[rows, block] * factor
        den[rows, block] = jnp.broadcast_to(factor, (size, HD))
        num[rows, block] = jnp.broadcast_to(top * factor * factor, (size, HD))
        return attn

    def settle_own(step, carry):
        tops = [inner(step * group + i, 0, 0) for i in range(group)]
        for i in range(group):
            block = step * group + i
            put(own_out, block, 0, settle(block, 0, den[0, block], tops[i]))
        return carry

    shared_rows = heavy.astype(jnp.int32)
    partner = (far + here, core)

    def st_copy():
        return remote(st_mine, st_got, st_sent, st_landed, partner)

    def measure_rows(block, carry):
        top = inner(block, shared_rows, 2 * shared_rows)
        total = den[shared_rows, block]
        return jnp.where(lane == block, total, jnp.where(lane == blocks + block, top, carry))

    def settle_shared(target):
        def body(step, carry):
            for i in range(group):
                block = step * group + i
                both = st_mine[...] + st_got[...]
                total = jnp.sum(jnp.where(lane == block, both, 0.0), axis=1, keepdims=True)
                top = jnp.sum(jnp.where(lane == blocks + block, both, 0.0), axis=1, keepdims=True)
                put(target, block, 0, settle(block, shared_rows, total, top))
            return carry

        return body

    def backward(block, which, rows, qi, ki, vi, gi):
        weights = e_ref[which, block]
        grads = (of(gv, gi, block, 0, HD).astype(jnp.float32) * den[rows, block]).astype(kind)
        product = dot(grads, of(gv, vi, block, 0, HD), 1, 1)
        delta = num[rows, block]
        slope = (weights.astype(jnp.float32) * (product - delta)).astype(kind)
        return (
            dot(slope, of(qk, ki, block, 0, HD), 1, 0) * inv,
            dot(slope, of(qk, qi, block, 0, HD), 0, 0) * inv,
            dot(weights, grads, 0, 0),
        )

    def back_light(step, carry):
        found = [backward(step * group + i, 0, 0, 0, 1, 1, 0) for i in range(group)]
        for i, grads in enumerate(found):
            for j in range(3):
                put(own_out, step * group + i, (j + 1) * HD, grads[j])
        return carry

    def back_heavy(step, carry):
        found = []
        for i in range(group):
            block = step * group + i
            found.append(
                (
                    backward(block, 0, 0, 0, 1, 1, 0),
                    backward(block, 1, cross_rows, cross_q, cross_k, cross_v, cross_g),
                )
            )
        share = core.astype(jnp.float32)
        for i, (near, away) in enumerate(found):
            block = step * group + i
            put(own_out, block, HD, near[0] + away[0] * share)
            put(own_out, block, 2 * HD, near[1] + away[1] * (1.0 - share))
            put(own_out, block, 3 * HD, near[2] + away[2] * (1.0 - share))

            @pl.when(first)
            def _(away=away, block=block):
                put(cross_out, block, HD, away[0])

            @pl.when(jnp.logical_not(first))
            def _(away=away, block=block):
                put(cross_out, block, 0, away[1])
                put(cross_out, block, HD, away[2])

        return carry

    def unpack(peer, ref, pair, low, high, index):
        both = ref[:, pair_rows(pair), low:high].astype(jnp.float32)
        part = both[:, index * cap : (index + 1) * cap, :].reshape(nslots, high - low)
        return dot(onehot_t[peer], part.astype(kind), 1, 0).astype(kind)

    def a_copy(head):
        return remote(
            stage_a.at[head], got_a.at[here], a_sent.at[head], a_landed.at[here],
            (base + head, core),
        )

    def g_copy(head):
        return remote(
            stage_g.at[head], got_g.at[here], g_sent.at[head], g_landed.at[here],
            (base + head, core),
        )

    def cx_copy(index, head):
        return remote(
            stage_x.at[index, head], got_x.at[index, here], cx_sent.at[index, head],
            cx_landed.at[index, here], (far + head, core),
        )

    def return_own(low, high, stage, got, copy):
        def body(step, carry):
            pair = lax.rem(here // 2 + step + 1, pairs)
            for index in range(2):
                target = 2 * pair + index
                stage[target] = unpack(base + target, own_out, pair, low, high, index)

                @pl.when(target != here)
                def _():
                    copy(target).start()

                @pl.when(target == here)
                def _():
                    got[target] = stage[target]

            return carry

        lax.fori_loop(0, pairs, body, 0)

    def return_cross(part):
        def body(step, carry):
            pair = lax.rem(here // 2 + step, pairs)
            for index in range(2):
                target = 2 * pair + index
                stage_x[part, target] = unpack(
                    far + target, cross_out, pair, part * HD, (part + 1) * HD, index
                )
                cx_copy(part, target).start()
            return carry

        lax.fori_loop(0, pairs, body, 0)

    lax.fori_loop(0, pairs, pack_own, 0)
    lax.fori_loop(0, blocks // group, diagonal, 0)

    @pl.when(heavy)
    def _():
        lax.fori_loop(0, pairs, pack_cross, 0)
        lax.fori_loop(0, blocks // group, across, 0)

    @pl.when(first)
    def _():
        st_mine[...] = lax.fori_loop(0, blocks, measure_rows, jnp.zeros((size, HD), jnp.float32))
        st_copy().start()

    @pl.when(jnp.logical_not(jnp.logical_and(first, light)))
    def _():
        lax.fori_loop(0, blocks // group, settle_own, 0)

    @pl.when(first)
    def _():
        st_copy().wait_recv()

        @pl.when(heavy)
        def _():
            lax.fori_loop(0, blocks // group, settle_shared(cross_out), 0)
            return_cross(0)

        @pl.when(light)
        def _():
            lax.fori_loop(0, blocks // group, settle_shared(own_out), 0)

    return_own(0, HD, stage_a, got_a, a_copy)

    @pl.when(light)
    def _():
        lax.fori_loop(0, blocks // group, back_light, 0)

    @pl.when(heavy)
    def _():
        lax.fori_loop(0, blocks // group, back_heavy, 0)

        @pl.when(jnp.logical_not(first))
        def _():
            return_cross(0)

        return_cross(1)

    return_own(HD, 4 * HD, stage_g, got_g, g_copy)

    piece = w_ref.shape[2]

    def w_swap(peer):
        return remote(
            w_ref.at[peer, other], w_held.at[peer], w_swap_sent.at[peer], w_swap_landed.at[peer],
            (chip, other),
        )

    def x_copy(j):
        return remote(
            x_stage.at[j], x_got.at[j], x_sent.at[j], x_landed.at[j], (chip + 1 - 2 * x, core)
        )

    def y_copy(j):
        return remote(
            y_stage.at[j], y_got.at[j], y_sent.at[j], y_landed.at[j], (chip + 2 - 4 * y, core)
        )

    def z_copy(j):
        return remote(
            z_stage.at[j], z_got.at[z], z_sent.at[j], z_landed.at[z], (4 * j + 2 * y + x, core)
        )

    def wait_cross(part, head):
        remote(
            stage_x.at[part, 0], got_x.at[part, head], cx_sent.at[part, 0],
            cx_landed.at[part, head], (chip, other),
        ).wait_recv()

    def term(step, carry):
        head = lax.rem(here + heads - step, heads)

        @pl.when(head != here)
        def _():
            remote(
                stage_a.at[0], got_a.at[head], a_sent.at[0], a_landed.at[head], (chip, other)
            ).wait_recv()

        @pl.when(jnp.logical_and(first, light))
        def _():
            wait_cross(0, head)
            a_ref[:, lanes(head)] = (
                got_a[head].astype(jnp.float32) + got_x[0, head].astype(jnp.float32)
            ).astype(kind)

        @pl.when(jnp.logical_not(jnp.logical_and(first, light)))
        def _():
            a_ref[:, lanes(head)] = got_a[head]

        total = dot(a_ref[:, lanes(head)], c_ref[...], 0, 0)
        for index in range(4):
            w_ref[2 * head + index // 2, index % 2] = total[
                index * piece : (index + 1) * piece
            ].astype(w_ref.dtype)
        w_swap(2 * head).start()
        w_swap(2 * head + 1).start()
        return carry

    def both_cores(peer):
        w_swap(peer).wait_recv()
        return w_ref[peer, core].astype(jnp.float32) + w_held[peer].astype(jnp.float32)

    def x_phase(j, carry):
        x_stage[j] = both_cores(2 * j + 1 - x).astype(x_stage.dtype)
        x_copy(j).start()
        kept[j] = both_cores(2 * j + x)
        return carry

    def y_phase(j, carry):
        away, stay = 2 * j + 1 - y, 2 * j + y
        x_copy(away).wait_recv()
        y_stage[j] = (kept[away] + x_got[away].astype(jnp.float32)).astype(y_stage.dtype)
        y_copy(j).start()
        x_copy(stay).wait_recv()
        kept[stay] += x_got[stay].astype(jnp.float32)
        return carry

    def z_phase(j, carry):
        y_copy(j).wait_recv()
        total = kept[2 * j + y] + y_got[j].astype(jnp.float32)

        @pl.when(j != z)
        def _():
            z_stage[j] = total.astype(z_stage.dtype)
            z_copy(j).start()

        @pl.when(j == z)
        def _():
            grad_ref[...] = total

        return carry

    def z_sum(j, carry):
        @pl.when(j != z)
        def _():
            remote(
                z_stage.at[j], z_got.at[j], z_sent.at[j], z_landed.at[j], (4 * j + 2 * y + x, core)
            ).wait_recv()
            grad_ref[...] += z_got[j].astype(jnp.float32)
            z_copy(j).wait_send()

        y_copy(j).wait_send()
        return carry

    def ends(j, carry):
        x_copy(j).wait_send()
        w_swap(2 * j).wait_send()
        w_swap(2 * j + 1).wait_send()
        return carry

    lax.fori_loop(0, heads, term, 0)
    lax.fori_loop(0, n // 2, x_phase, 0)

    depth = w_full.shape[1]
    tile = 2 * HD

    def project(step, carry):
        columns = pl.ds(pl.multiple_of(step * tile, tile), tile)
        total = jnp.dot(
            a_ref[:, :depth], w_full[0, :, columns], preferred_element_type=jnp.float32
        ) + jnp.dot(a_ref[:, depth:], w_full[1, :, columns], preferred_element_type=jnp.float32)
        out_ref[:, columns] = total.astype(out_ref.dtype)
        return carry

    lax.fori_loop(0, out_ref.shape[1] // tile, project, 0)
    lax.fori_loop(0, quarter, y_phase, 0)

    def finish(step, carry):
        head = lax.rem(here + heads - step, heads)

        @pl.when(head != here)
        def _():
            remote(
                stage_g.at[0], got_g.at[head], g_sent.at[0], g_landed.at[head], (chip, other)
            ).wait_recv()

        grads = [got_g[head, :, i * HD : (i + 1) * HD].astype(jnp.float32) for i in range(3)]

        @pl.when(light)
        def _():
            wait_cross(1, head)

            @pl.when(jnp.logical_not(first))
            def _():
                wait_cross(0, head)

        extra = [
            jnp.where(light, got_x[i, head].astype(jnp.float32), 0.0) for i in range(2)
        ]
        grads[0] = grads[0] + jnp.where(first, extra[1], 0.0)
        grads[1] = grads[1] + jnp.where(first, 0.0, extra[0])
        grads[2] = grads[2] + jnp.where(first, 0.0, extra[1])
        for gradient, source, target in ((grads[0], q_ref, gq_ref), (grads[1], k_ref, gk_ref)):
            normed, factor = normalize(source[:, lanes(head)])
            mean = jnp.mean(gradient * normed, axis=-1, keepdims=True)
            target[:, lanes(head)] = (factor * (gradient - normed * mean)).astype(target.dtype)
        gv_ref[:, lanes(head)] = grads[2].astype(gv_ref.dtype)
        return carry

    lax.fori_loop(0, quarter, z_phase, 0)
    lax.fori_loop(0, heads, finish, 0)
    lax.fori_loop(0, quarter, z_sum, 0)
    grad_ref[...] = grad_ref[...] * scale
    lax.fori_loop(0, n // 2, ends, 0)

    def sends_done(head, carry):
        @pl.when(head != here)
        def _():
            id_copy(base + head).wait_send()
            data_copy(head).wait_send()
            a_copy(head).wait_send()
            g_copy(head).wait_send()

        @pl.when(light)
        def _():
            id_copy(far + head).wait_send()
            cross_copy(head).wait_send()

        @pl.when(heavy)
        def _():
            cx_copy(0, head).wait_send()
            cx_copy(1, head).wait_send()

        return carry

    lax.fori_loop(0, heads, sends_done, 0)
    w_copy.wait_send()

    @pl.when(first)
    def _():
        st_copy().wait_send()


def layer_call(q, k, v, c, w, labels, clusters, scale):
    tokens, features = q.shape
    heads = features // HD
    n = 2 * heads
    rows = heads * (2 * tokens // clusters)
    blocks = clusters // 2
    kind = q.dtype
    wide = jnp.float32
    vmem = pl.BlockSpec(memory_space=pltpu.VMEM)
    piece = (features // (2 * n), c.shape[1])
    like = jax.ShapeDtypeStruct(q.shape, kind)
    nslots = 2 * tokens
    pair = 2 * rows
    buffers = [
        (q.shape, kind), (q.shape, kind), (q.shape, kind), (c.shape, kind),
        ((2,) + w.shape, kind),
        ((heads, tokens, 4 * HD), kind),
        ((heads, tokens, 4 * HD), kind),
        ((heads, tokens, 2 * HD), kind),
        ((8, tokens), wide),
        ((n, 8, tokens), wide),
        ((n, tokens, nslots), kind),
        ((3, clusters, rows, HD), kind),
        ((3, clusters, rows, 2 * HD), kind),
        ((2, blocks, pair, pair), kind),
        ((2, blocks, pair, HD), wide),
        ((2, blocks, pair, HD), wide),
        ((clusters, rows, 4 * HD), kind),
        ((clusters, rows, 2 * HD), kind),
        ((pair, HD), wide),
        ((pair, HD), wide),
        ((heads, tokens, HD), kind),
        ((heads, tokens, 3 * HD), kind),
        ((2, heads, tokens, HD), kind),
        ((heads, tokens, HD), kind),
        ((heads, tokens, 3 * HD), kind),
        ((2, heads, tokens, HD), kind),
        (q.shape, kind),
        ((n, 2) + piece, kind),
        ((n,) + piece, kind),
        ((n // 2,) + piece, wide),
        ((n // 2,) + piece, kind),
        ((n // 2,) + piece, kind),
    ] + [((n // 4,) + piece, kind)] * 4
    one = pltpu.SemaphoreType.DMA

    def many(*count):
        return pltpu.SemaphoreType.DMA(count)

    semaphores = (
        [many(5), one, one, many(heads), many(heads), many(heads), many(heads), many(n), many(n)]
        + [one, one]
        + [many(heads)] * 4
        + [many(2, heads)] * 2
        + [many(n)] * 2
        + [many(n // 2)] * 2
        + [many(n // 4)] * 4
    )
    return pl.pallas_call(
        functools.partial(layer_kernel, heads, scale),
        out_shape=(
            like, like, like, jax.ShapeDtypeStruct(c.shape, kind),
            jax.ShapeDtypeStruct(piece, wide),
        ),
        in_specs=[pl.BlockSpec(memory_space=pl.ANY)] * 5 + [vmem],
        out_specs=(vmem,) * 5,
        scratch_shapes=[pltpu.VMEM(shape, dtype) for shape, dtype in buffers] + semaphores,
        compiler_params=pltpu.CompilerParams(
            collective_id=0, has_side_effects=True, vmem_limit_bytes=60 << 20
        ),
    )(q, k, v, c, w, labels)


def per_device_heads(queries, key_rows, value_rows, cotangent, w_out, cluster_ids):
    tokens = queries.shape[1]
    seq_devices = lax.axis_size("seq")
    scale = 1.0 / math.sqrt(tokens * seq_devices * 2)
    grad_queries, grad_keys, grad_values, projected, weight_grad = layer_call(
        queries[0], key_rows[0], value_rows[0], cotangent[0], w_out, cluster_ids,
        CL_DEV * seq_devices, scale,
    )
    return (projected[None], grad_queries[None], grad_keys[None], grad_values[None], weight_grad)


def per_device(queries, *rest):
    heads = queries.shape[2] // HD
    if lax.axis_size("dp") == 2 and lax.axis_size("seq") == 2 * heads:
        return per_device_heads(queries, *rest)
    return per_device_slots(queries, *rest)


def solution(mesh):
    in_specs = (
        P("dp", "seq", None),
        P("dp", "seq", None),
        P("dp", "seq", None),
        P("dp", "seq", None),
        P("dp", None),
        P("dp", "seq"),
    )
    out_specs = (
        P("dp", "seq", None),
        P("dp", "seq", None),
        P("dp", "seq", None),
        P("dp", "seq", None),
        P(("seq", "dp"), None),
    )
    return jax.shard_map(
        per_device, mesh=mesh, in_specs=in_specs, out_specs=out_specs, check_vma=False
    )
```

time: 149 us -> 138 us (0.926)
  matrix products: 13.5 us -> 0 us
  Pallas kernels: 118 us -> 131 us
  local copies, waits for them, and re-layouts: 12.8 us -> 6.07 us
  other arithmetic: 2.36 us -> 0 us
    pallas_call x2 -> x1, Pallas kernels: 118 us -> 131 us  [layer_call(): pl.pallas_call(functools.partial(layer_kernel, heads, scale), out_shape=(...]
    dot_general x8 -> x0, matrix products: 10.2 us -> none  [the longest x2 4.24 us: take(): jnp.einsum('dspt,dsf->pdtf', one_hot.reshape(seq_devices, my_slots, 2, ha...]
    unnamed x26 -> x13, local copies, waits for them, and re-layouts: 9.93 us -> 6.07 us
    div x1 -> x0, matrix products: 3.27 us -> none  [attend(): probs = weights / jnp.sum(weights, axis=-1, keepdims=True)]
    transpose x1 -> x0, local copies, waits for them, and re-layouts: 2.49 us -> none  [per_device_heads(): packed = jnp.transpose(packed, (1, 0, 2, 3))]
    reduce_sum x2 -> x0, other arithmetic: 1.63 us -> none  [the longest x1 0.93 us: per_device_heads(): ranks = jnp.sum(jnp.logical_and(matching, earlier), axis=1)]
where the time goes in v1:
time: 138 us
  Pallas kernels  131 us (95%)
  local copies, waits for them, and re-layouts  6.07 us (4%)
    pallas_call x1, Pallas kernels, layer_call(): pl.pallas_call(functools.partial(layer_kernel, heads, scale), out_shape=(...  131 us
    unnamed x13, local copies, waits for them, and re-layouts  6.07 us

profile of v1, /device:TPU:0, one launch (start us, length us, event | category | flops | bytes accessed | tf_op | source)
XLA Modules:
  0.0 137.7 jit_solution(7317854212119375789)
XLA Ops:
  0.6 131.0 %shard_map.101 = (bf16[256,1024]{1,0:T(8,128)(2,1)}, bf16[256,1024]{1,0:T(8,128)(2,1)}, bf16[256,1024]{1,0:T(8,128)(2,1)}, bf16[256,1024]{1,0:T(8,128)(2,1)}, f32[32,1024]{1,0:T(8,128)}) custom-call(bf16[256,1024]{1,0:T(8,128)(2,1)} %bitcast.12, bf16[256,1024]{1,0:T(8,128)(2,1)} %bitcast.13, bf16[256,1024]{1,0:T(8,128)(2,1)} %bitcast.14, ...), custom_call_target="tpu_custom_call" | custom-call | tf_op jit(solution)/shard_map/pallas_call | solution.py:864
  131.6 0.0 copy-start.2
  131.6 1.9 %copy.16 = bf16[1,256,1024]{2,1,0:T(8,128)(2,1)} copy(bf16[1,256,1024]{2,1,0:T(8,128)(2,1)} %bitcast.11) | data formatting | bytes 1048576
  133.6 0.0 copy-done.2
  133.6 0.0 copy-start.1
  133.6 0.8 copy.17
  134.4 0.4 copy-done.1
  134.8 0.0 copy-start
  134.8 0.8 copy.18
  135.6 0.4 copy-done
  136.0 0.0 copy-start.3
  136.0 0.8 copy.19
  136.8 0.2 copy-done.3
  137.0 0.7 copy.20
Async XLA Ops:
  131.6 1.9 %copy-start.2 = (bf16[256,1024]{1,0:T(8,128)(2,1)S(1)}, bf16[256,1024]{1,0:T(8,128)(2,1)}, u32[]{:S(2)}) copy-start(bf16[256,1024]{1,0:T(8,128)(2,1)} %get-tuple-element.11) | copy-start | bytes 1572868
  133.6 1.2 copy-start.1
  134.8 1.2 copy-start
  136.0 1.0 copy-start.3

commit v2 on v1

--- a/solution.py
+++ b/solution.py
@@ -180,12 +180,13 @@
 def layer_kernel(
     heads, scale,
     q_in, k_in, v_in, c_in, w_in, labels_ref,
+    gq_out, gk_out, gv_out, out_out, grad_out,
     gq_ref, gk_ref, gv_ref, out_ref, grad_ref,
     q_ref, k_ref, v_ref, c_ref, w_full, x_ref, full, xfull, ids_ref, slots,
-    onehot_t, qk, gv, e_ref, num, den, own_out, cross_out, st_mine, st_got,
+    onehot_t, allow_ref, qk, gv, e_ref, num, den, own_out, cross_out, st_mine, st_got,
     stage_a, stage_g, stage_x, got_a, got_g, got_x,
     a_ref, w_ref, w_held, kept, x_stage, x_got, y_stage, y_got, z_stage, z_got,
-    loaded, w_sent, w_landed, sent, landed, xsent, xlanded, id_sent, id_landed, st_sent, st_landed,
+    stored, stored_heads, loaded, w_sent, w_landed, sent, landed, xsent, xlanded, id_sent, id_landed, st_sent, st_landed,
     a_sent, a_landed, g_sent, g_landed, cx_sent, cx_landed,
     w_swap_sent, w_swap_landed, x_sent, x_landed, y_sent, y_landed, z_sent, z_landed,
 ):
@@ -208,6 +209,16 @@
     cap = rows_of // heads
     nslots = clusters * cap
     inv = 1.0 / math.sqrt(HD)
+    zl = here // 4
+    near_first = zl == core
+
+    def toward(mask_a, mask_b):
+        x_bit, y_bit, z_bit = [
+            jnp.where(near_first, (mask_a >> b) & 1, (mask_b >> b) & 1) for b in range(3)
+        ]
+        return lax.rem(zl + z_bit, 2) * 4 + lax.rem(y + y_bit, 2) * 2 + lax.rem(x + x_bit, 2)
+
+    order = tuple(zip((3, 1, 2, 0, 4, 6, 5, 7), (4, 6, 5, 7, 3, 1, 2, 0)))
 
     ins = ((q_in, q_ref), (k_in, k_ref), (v_in, v_ref), (c_in, c_ref), (w_in, w_full.at[core]))
     loads = [
@@ -275,34 +286,38 @@
 
     per_core = heads // 2
 
-    def prepare(step, carry):
-        head = lax.rem(here + step + 1, heads)
+    def prepare(head):
         x_ref[head, :, 0:HD] = normalize(q_ref[:, lanes(head)])[0].astype(kind)
         x_ref[head, :, 2 * HD : 3 * HD] = normalize(k_ref[:, lanes(head)])[0].astype(kind)
         x_ref[head, :, 3 * HD : 4 * HD] = v_ref[:, lanes(head)]
-
-        @pl.when(step == 0)
-        def _():
-            remote(w_in, w_full.at[other], w_sent, w_landed, (chip, other)).wait_recv()
-
         w_rows = w_full[head // per_core, lanes(lax.rem(head, per_core)), :]
         x_ref[head, :, HD : 2 * HD] = dot(c_ref[...], w_rows, 1, 1).astype(kind)
 
+    def send_data(head):
+        @pl.when(head != here)
+        def _():
+            data_copy(head).start()
+
+    for step, masks in enumerate(order):
+        head = toward(*masks)
+        if step == per_core:
+            remote(w_in, w_full.at[other], w_sent, w_landed, (chip, other)).wait_recv()
+        prepare(head)
+
         @pl.when(light)
-        def _():
+        def _(head=head):
             cross_copy(head).start()
 
-        @pl.when(step < heads - 1)
-        def _():
-            data_copy(head).start()
-
-        @pl.when(step == heads - 1)
-        def _():
-            full[here] = x_ref[here]
-
-        return carry
-
-    lax.fori_loop(0, heads, prepare, 0)
+        @pl.when(heavy)
+        def _(head=head):
+            send_data(head)
+
+    @pl.when(light)
+    def _():
+        for masks in order:
+            send_data(toward(*masks))
+
+    full[here] = x_ref[here]
 
     def wait_ids(peer):
         remote(ids_ref, slots.at[peer], id_sent.at[0], id_landed.at[peer], (chip, other)).wait_recv()
@@ -321,8 +336,13 @@
     def pair_rows(pair):
         return pl.ds(pl.multiple_of(pair * 2 * cap, 2 * cap), 2 * cap)
 
+    def pair_toward(step):
+        z_bit = lax.rem(step // 2 + jnp.where(near_first, 0, 1), 2)
+        y_bit = lax.rem(step + jnp.where(near_first, 1, 0) * (1 - step // 2), 2)
+        return lax.rem(zl + z_bit, 2) * 2 + lax.rem(y + y_bit, 2)
+
     def pack_own(step, carry):
-        pair = lax.rem(here // 2 + pairs - step, pairs)
+        pair = pair_toward(step)
         parts, valids = [], []
         for index in range(2):
             source = 2 * pair + index
@@ -347,7 +367,7 @@
         return carry
 
     def pack_cross(step, carry):
-        pair = lax.rem(here // 2 + pairs - step, pairs)
+        pair = pair_toward(step)
         parts, valids = [], []
         for index in range(2):
             source = 2 * pair + index
@@ -370,10 +390,11 @@
     down = lax.broadcasted_iota(jnp.int32, (size, size), 0)
     along = lax.broadcasted_iota(jnp.int32, (size, size), 1)
     lane = lax.broadcasted_iota(jnp.int32, (size, HD), 1)
-    group = 2
-
-    def one_cluster():
-        return down // rows_of == along // rows_of
+    group = 4
+
+    one_cluster = (down < rows_of) == (along < rows_of)
+    allow_ref[0] = jnp.where(jnp.logical_and(one_cluster, along <= down), 1.0, 0.0)
+    allow_ref[1] = jnp.where(one_cluster, 1.0, 0.0)
 
     def of(ref, index, block, low, high):
         part = ref[index, pl.ds(2 * block, 2), :, low:high]
@@ -387,75 +408,92 @@
 
     def forward(block, qi, ki, vi, allowed):
         scores = dot(of(qk, qi, block, 0, HD), of(qk, ki, block, 0, HD), 1, 1)
-        weights = jnp.where(allowed, jnp.exp(scores * inv), 0.0).astype(kind)
+        weights = (jnp.exp(scores * inv) * allow_ref[allowed]).astype(kind)
         both = dot(weights, of(gv, vi, block, 0, 2 * HD), 1, 0)
         return weights, both[:, :HD], both[:, HD:]
 
-    def diagonal(step, carry):
-        allowed = jnp.logical_and(one_cluster(), along <= down)
-        found = [forward(step * group + i, 0, 1, 1, allowed) for i in range(group)]
-        for i, (weights, top, total) in enumerate(found):
-            e_ref[0, step * group + i] = weights
-            num[0, step * group + i] = top
-            den[0, step * group + i] = total
-        return carry
+    def inner(block, grads, top):
+        return jnp.sum(
+            of(gv, grads, block, 0, HD).astype(jnp.float32) * top, axis=1, keepdims=True
+        )
+
+    def settle(target, block, rows, top, total, product):
+        factor = 1.0 / jnp.where(total > 0, total, 1.0)
+        den[rows, block] = jnp.broadcast_to(factor, (size, HD))
+        num[rows, block] = jnp.broadcast_to(product * (factor * factor), (size, HD))
+        put(target, block, 0, top * factor)
+
+    def sums(carry, block, total, product):
+        return jnp.where(lane == block, total, jnp.where(lane == blocks + block, product, carry))
 
     cross_rows = other
     cross_q, cross_k = 2 * other, 1 + core
     cross_g, cross_v = 2 * other, 1 + core
-
-    def across(step, carry):
-        found = []
-        for i in range(group):
-            block = step * group + i
-            weights, top, total = forward(block, cross_q, cross_k, cross_v, one_cluster())
-            share = core.astype(jnp.float32)
-            found.append((weights, top + num[0, block] * share, total + den[0, block] * share))
-        for i, (weights, top, total) in enumerate(found):
-            e_ref[1, step * group + i] = weights
-            num[cross_rows, step * group + i] = top
-            den[cross_rows, step * group + i] = total
-        return carry
-
-    def inner(block, rows, grads):
-        return jnp.sum(
-            of(gv, grads, block, 0, HD).astype(jnp.float32) * num[rows, block],
-            axis=1, keepdims=True,
-        )
-
-    def settle(block, rows, total, top):
-        factor = 1.0 / jnp.where(total > 0, total, 1.0)
-        attn = num[rows, block] * factor
-        den[rows, block] = jnp.broadcast_to(factor, (size, HD))
-        num[rows, block] = jnp.broadcast_to(top * factor * factor, (size, HD))
-        return attn
-
-    def settle_own(step, carry):
-        tops = [inner(step * group + i, 0, 0) for i in range(group)]
-        for i in range(group):
-            block = step * group + i
-            put(own_out, block, 0, settle(block, 0, den[0, block], tops[i]))
-        return carry
-
     shared_rows = heavy.astype(jnp.int32)
-    partner = (far + here, core)
+
+    def each(step, one):
+        return [one(step * group + i) for i in range(group)]
+
+    def diagonal_whole(step, carry):
+        def one(block):
+            weights, top, total = forward(block, 0, 1, 1, 0)
+            return block, weights, top, total, inner(block, 0, top)
+
+        for block, weights, top, total, product in each(step, one):
+            e_ref[0, block] = weights
+            settle(own_out, block, 0, top, total, product)
+        return carry
+
+    def diagonal_part(step, carry):
+        def one(block):
+            weights, top, total = forward(block, 0, 1, 1, 0)
+            return block, weights, top, total, inner(block, 0, top)
+
+        for block, weights, top, total, product in each(step, one):
+            e_ref[0, block] = weights
+            num[0, block] = top
+            den[0, block] = total
+            carry = sums(carry, block, total, product)
+        return carry
+
+    def across_keys(step, carry):
+        def one(block):
+            weights, top, total = forward(block, 0, 2, 2, 1)
+            top, total = top + num[0, block], total + den[0, block]
+            return block, weights, top, total, inner(block, 0, top)
+
+        for block, weights, top, total, product in each(step, one):
+            e_ref[1, block] = weights
+            settle(own_out, block, 0, top, total, product)
+        return carry
+
+    def across_queries(step, carry):
+        def one(block):
+            weights, top, total = forward(block, 2, 1, 1, 1)
+            return block, weights, top, total, inner(block, 2, top)
+
+        for block, weights, top, total, product in each(step, one):
+            e_ref[1, block] = weights
+            num[1, block] = top
+            carry = sums(carry, block, total, product)
+        return carry
 
     def st_copy():
-        return remote(st_mine, st_got, st_sent, st_landed, partner)
-
-    def measure_rows(block, carry):
-        top = inner(block, shared_rows, 2 * shared_rows)
-        total = den[shared_rows, block]
-        return jnp.where(lane == block, total, jnp.where(lane == blocks + block, top, carry))
+        return remote(st_mine, st_got, st_sent, st_landed, (far + here, core))
 
     def settle_shared(target):
         def body(step, carry):
-            for i in range(group):
-                block = step * group + i
-                both = st_mine[...] + st_got[...]
+            both = st_mine[...] + st_got[...]
+
+            def one(block):
                 total = jnp.sum(jnp.where(lane == block, both, 0.0), axis=1, keepdims=True)
-                top = jnp.sum(jnp.where(lane == blocks + block, both, 0.0), axis=1, keepdims=True)
-                put(target, block, 0, settle(block, shared_rows, total, top))
+                product = jnp.sum(
+                    jnp.where(lane == blocks + block, both, 0.0), axis=1, keepdims=True
+                )
+                return block, num[shared_rows, block], total, product
+
+            for block, top, total, product in each(step, one):
+                settle(target, block, shared_rows, top, total, product)
             return carry
 
         return body
@@ -532,7 +570,7 @@
 
     def return_own(low, high, stage, got, copy):
         def body(step, carry):
-            pair = lax.rem(here // 2 + step + 1, pairs)
+            pair = pair_toward(step)
             for index in range(2):
                 target = 2 * pair + index
                 stage[target] = unpack(base + target, own_out, pair, low, high, index)
@@ -551,7 +589,7 @@
 
     def return_cross(part):
         def body(step, carry):
-            pair = lax.rem(here // 2 + step, pairs)
+            pair = pair_toward(step)
             for index in range(2):
                 target = 2 * pair + index
                 stage_x[part, target] = unpack(
@@ -562,35 +600,43 @@
 
         lax.fori_loop(0, pairs, body, 0)
 
+    rounds = blocks // group
+    nothing = jnp.zeros((size, HD), jnp.float32)
     lax.fori_loop(0, pairs, pack_own, 0)
-    lax.fori_loop(0, blocks // group, diagonal, 0)
+
+    @pl.when(heavy == first)
+    def _():
+        lax.fori_loop(0, rounds, diagonal_whole, 0)
+
+    @pl.when(heavy != first)
+    def _():
+        st_mine[...] = lax.fori_loop(0, rounds, diagonal_part, nothing)
 
     @pl.when(heavy)
     def _():
         lax.fori_loop(0, pairs, pack_cross, 0)
-        lax.fori_loop(0, blocks // group, across, 0)
+
+        @pl.when(jnp.logical_not(first))
+        def _():
+            lax.fori_loop(0, rounds, across_keys, 0)
+
+        @pl.when(first)
+        def _():
+            st_mine[...] = lax.fori_loop(0, rounds, across_queries, nothing)
 
     @pl.when(first)
     def _():
-        st_mine[...] = lax.fori_loop(0, blocks, measure_rows, jnp.zeros((size, HD), jnp.float32))
         st_copy().start()
-
-    @pl.when(jnp.logical_not(jnp.logical_and(first, light)))
-    def _():
-        lax.fori_loop(0, blocks // group, settle_own, 0)
-
-    @pl.when(first)
-    def _():
         st_copy().wait_recv()
 
         @pl.when(heavy)
         def _():
-            lax.fori_loop(0, blocks // group, settle_shared(cross_out), 0)
+            lax.fori_loop(0, rounds, settle_shared(cross_out), 0)
             return_cross(0)
 
         @pl.when(light)
         def _():
-            lax.fori_loop(0, blocks // group, settle_shared(own_out), 0)
+            lax.fori_loop(0, rounds, settle_shared(own_out), 0)
 
     return_own(0, HD, stage_a, got_a, a_copy)
 
@@ -618,14 +664,24 @@
             (chip, other),
         )
 
+    turn, turn_next = jnp.where(first, x, y), jnp.where(first, y, x)
+    step_x, step_y = chip + 1 - 2 * x, chip + 2 - 4 * y
+
+    def piece_of(j, bit):
+        return (j // 2) * 4 + jnp.where(
+            first, 2 * lax.rem(j, 2) + bit, lax.rem(j, 2) + 2 * bit
+        )
+
     def x_copy(j):
         return remote(
-            x_stage.at[j], x_got.at[j], x_sent.at[j], x_landed.at[j], (chip + 1 - 2 * x, core)
+            x_stage.at[j], x_got.at[j], x_sent.at[j], x_landed.at[j],
+            (jnp.where(first, step_x, step_y), core),
         )
 
     def y_copy(j):
         return remote(
-            y_stage.at[j], y_got.at[j], y_sent.at[j], y_landed.at[j], (chip + 2 - 4 * y, core)
+            y_stage.at[j], y_got.at[j], y_sent.at[j], y_landed.at[j],
+            (jnp.where(first, step_y, step_x), core),
         )
 
     def z_copy(j):
@@ -673,13 +729,13 @@
         return w_ref[peer, core].astype(jnp.float32) + w_held[peer].astype(jnp.float32)
 
     def x_phase(j, carry):
-        x_stage[j] = both_cores(2 * j + 1 - x).astype(x_stage.dtype)
+        x_stage[j] = both_cores(piece_of(j, 1 - turn)).astype(x_stage.dtype)
         x_copy(j).start()
-        kept[j] = both_cores(2 * j + x)
+        kept[j] = both_cores(piece_of(j, turn))
         return carry
 
     def y_phase(j, carry):
-        away, stay = 2 * j + 1 - y, 2 * j + y
+        away, stay = 2 * j + 1 - turn_next, 2 * j + turn_next
         x_copy(away).wait_recv()
         y_stage[j] = (kept[away] + x_got[away].astype(jnp.float32)).astype(y_stage.dtype)
         y_copy(j).start()
@@ -689,7 +745,7 @@
 
     def z_phase(j, carry):
         y_copy(j).wait_recv()
-        total = kept[2 * j + y] + y_got[j].astype(jnp.float32)
+        total = kept[2 * j + turn_next] + y_got[j].astype(jnp.float32)
 
         @pl.when(j != z)
         def _():
@@ -735,7 +791,17 @@
         return carry
 
     lax.fori_loop(0, out_ref.shape[1] // tile, project, 0)
+    keep_out = pltpu.make_async_copy(out_ref, out_out, stored.at[0])
+    keep_out.start()
     lax.fori_loop(0, quarter, y_phase, 0)
+
+    results = ((gq_ref, gq_out), (gk_ref, gk_out), (gv_ref, gv_out))
+
+    def keep(index, head):
+        source, target = results[index]
+        return pltpu.make_async_copy(
+            source.at[:, lanes(head)], target.at[:, lanes(head)], stored_heads.at[index, head]
+        )
 
     def finish(step, carry):
         head = lax.rem(here + heads - step, heads)
@@ -767,15 +833,22 @@
             mean = jnp.mean(gradient * normed, axis=-1, keepdims=True)
             target[:, lanes(head)] = (factor * (gradient - normed * mean)).astype(target.dtype)
         gv_ref[:, lanes(head)] = grads[2].astype(gv_ref.dtype)
+        for index in range(3):
+            keep(index, head).start()
         return carry
 
     lax.fori_loop(0, quarter, z_phase, 0)
     lax.fori_loop(0, heads, finish, 0)
     lax.fori_loop(0, quarter, z_sum, 0)
     grad_ref[...] = grad_ref[...] * scale
+    keep_grad = pltpu.make_async_copy(grad_ref, grad_out, stored.at[1])
+    keep_grad.start()
     lax.fori_loop(0, n // 2, ends, 0)
 
     def sends_done(head, carry):
+        for index in range(3):
+            keep(index, head).wait()
+
         @pl.when(head != here)
         def _():
             id_copy(base + head).wait_send()
@@ -797,6 +870,8 @@
 
     lax.fori_loop(0, heads, sends_done, 0)
     w_copy.wait_send()
+    keep_out.wait()
+    keep_grad.wait()
 
     @pl.when(first)
     def _():
@@ -816,7 +891,8 @@
     like = jax.ShapeDtypeStruct(q.shape, kind)
     nslots = 2 * tokens
     pair = 2 * rows
-    buffers = [
+    buffers = [(q.shape, kind)] * 3 + [
+        (c.shape, kind), (piece, wide),
         (q.shape, kind), (q.shape, kind), (q.shape, kind), (c.shape, kind),
         ((2,) + w.shape, kind),
         ((heads, tokens, 4 * HD), kind),
@@ -825,6 +901,7 @@
         ((8, tokens), wide),
         ((n, 8, tokens), wide),
         ((n, tokens, nslots), kind),
+        ((2, pair, pair), wide),
         ((3, clusters, rows, HD), kind),
         ((3, clusters, rows, 2 * HD), kind),
         ((2, blocks, pair, pair), kind),
@@ -853,7 +930,7 @@
         return pltpu.SemaphoreType.DMA(count)
 
     semaphores = (
-        [many(5), one, one, many(heads), many(heads), many(heads), many(heads), many(n), many(n)]
+        [many(2), many(3, heads), many(5), one, one, many(heads), many(heads), many(heads), many(heads), many(n), many(n)]
         + [one, one]
         + [many(heads)] * 4
         + [many(2, heads)] * 2
@@ -868,7 +945,7 @@
             jax.ShapeDtypeStruct(piece, wide),
         ),
         in_specs=[pl.BlockSpec(memory_space=pl.ANY)] * 5 + [vmem],
-        out_specs=(vmem,) * 5,
+        out_specs=(pl.BlockSpec(memory_space=pl.ANY),) * 5,
         scratch_shapes=[pltpu.VMEM(shape, dtype) for shape, dtype in buffers] + semaphores,
         compiler_params=pltpu.CompilerParams(
             collective_id=0, has_side_effects=True, vmem_limit_bytes=60 << 20
@@ -876,14 +953,41 @@
     )(q, k, v, c, w, labels)
 
 
+def hand_over_kernel(count, *refs):
+    sources, targets, held = refs[:count], refs[count : 2 * count], refs[2 * count : 3 * count]
+    done_in, done_out = refs[3 * count :]
+    loads = [pltpu.make_async_copy(sources[i], held[i], done_in.at[i]) for i in range(count)]
+    stores = [pltpu.make_async_copy(held[i], targets[i], done_out.at[i]) for i in range(count)]
+    for load in loads:
+        load.start()
+    for load, store in zip(loads, stores):
+        load.wait()
+        store.start()
+    for store in stores:
+        store.wait()
+
+
+def hand_over(*arrays):
+    anywhere = pl.BlockSpec(memory_space=pl.ANY)
+    count = len(arrays)
+    return pl.pallas_call(
+        functools.partial(hand_over_kernel, count),
+        out_shape=tuple(jax.ShapeDtypeStruct(a.shape, a.dtype) for a in arrays),
+        in_specs=[anywhere] * count,
+        out_specs=(anywhere,) * count,
+        scratch_shapes=[pltpu.VMEM(a.shape, a.dtype) for a in arrays]
+        + [pltpu.SemaphoreType.DMA((count,))] * 2,
+    )(*arrays)
+
+
 def per_device_heads(queries, key_rows, value_rows, cotangent, w_out, cluster_ids):
     tokens = queries.shape[1]
     seq_devices = lax.axis_size("seq")
     scale = 1.0 / math.sqrt(tokens * seq_devices * 2)
-    grad_queries, grad_keys, grad_values, projected, weight_grad = layer_call(
+    grad_queries, grad_keys, grad_values, projected, weight_grad = hand_over(*layer_call(
         queries[0], key_rows[0], value_rows[0], cotangent[0], w_out, cluster_ids,
         CL_DEV * seq_devices, scale,
-    )
+    ))
     return (projected[None], grad_queries[None], grad_keys[None], grad_values[None], weight_grad)
 
 

time: 138 us -> 117 us (0.85); the launches traced: 138 us -> 115 us
  Pallas kernels: 131 us -> 115 us
  local copies, waits for them, and re-layouts: 6.07 us -> 0 us
    pallas_call x1, Pallas kernels: 131 us -> 112 us  [layer_call(): pl.pallas_call(functools.partial(layer_kernel, heads, scale), out_shape=(...]
    unnamed x13 -> x0, local copies, waits for them, and re-layouts: 6.07 us -> none
    pallas_call x0 -> x1, Pallas kernels: none -> 2.47 us  [hand_over(): pl.pallas_call(functools.partial(hand_over_kernel, count), out_shape=tupl...]
where the time goes in v2:
time: 117 us; the launch traced here: 115 us
  Pallas kernels  115 us (98%)
    pallas_call x1, Pallas kernels, layer_call(): pl.pallas_call(functools.partial(layer_kernel, heads, scale), out_shape=(...  112 us
    pallas_call x1, Pallas kernels, hand_over(): pl.pallas_call(functools.partial(hand_over_kernel, count), out_shape=tupl...  2.47 us

profile of v2, /device:TPU:0, one launch (start us, length us, event | category | flops | bytes accessed | tf_op | source)
XLA Modules:
  0.0 115.2 jit_solution(1734781691063558613)
XLA Ops:
  0.6 112.1 %shard_map.101 = (bf16[256,1024]{1,0:T(8,128)(2,1)}, bf16[256,1024]{1,0:T(8,128)(2,1)}, bf16[256,1024]{1,0:T(8,128)(2,1)}, bf16[256,1024]{1,0:T(8,128)(2,1)}, f32[32,1024]{1,0:T(8,128)}) custom-call(bf16[256,1024]{1,0:T(8,128)(2,1)} %bitcast.8, bf16[256,1024]{1,0:T(8,128)(2,1)} %bitcast.9, bf16[256,1024]{1,0:T(8,128)(2,1)} %bitcast.10, ...), custom_call_target="tpu_custom_call" | custom-call | tf_op jit(solution)/shard_map/pallas_call | solution.py:941
  112.8 2.5 %shard_map.102 = (bf16[256,1024]{1,0:T(8,128)(2,1)}, bf16[256,1024]{1,0:T(8,128)(2,1)}, bf16[256,1024]{1,0:T(8,128)(2,1)}, bf16[256,1024]{1,0:T(8,128)(2,1)}, f32[32,1024]{1,0:T(8,128)}) custom-call(bf16[256,1024]{1,0:T(8,128)(2,1)} %get-tuple-element.15.refs_0_, bf16[256,1024]{1,0:T(8,128)(2,1)} %get-tuple-element.16.refs_1_, ...), custom_call_target="tpu_custom_call" | custom-call | tf_op jit(solution)/shard_map/pallas_call | solution.py:973

commit v3 on v2

--- a/solution.py
+++ b/solution.py
@@ -183,11 +183,11 @@
     gq_out, gk_out, gv_out, out_out, grad_out,
     gq_ref, gk_ref, gv_ref, out_ref, grad_ref,
     q_ref, k_ref, v_ref, c_ref, w_full, x_ref, full, xfull, ids_ref, slots,
-    onehot_t, allow_ref, qk, gv, e_ref, num, den, own_out, cross_out, st_mine, st_got,
+    onehot_t, onehot, allow_ref, qk, gv, e_ref, num, den, own_out, cross_out, st_mine, st_got,
     stage_a, stage_g, stage_x, got_a, got_g, got_x,
     a_ref, w_ref, w_held, kept, x_stage, x_got, y_stage, y_got, z_stage, z_got,
     stored, stored_heads, loaded, w_sent, w_landed, sent, landed, xsent, xlanded, id_sent, id_landed, st_sent, st_landed,
-    a_sent, a_landed, g_sent, g_landed, cx_sent, cx_landed,
+    a_sent, a_landed, g_sent, g_landed, v_sent, v_landed, cx_sent, cx_landed,
     w_swap_sent, w_swap_landed, x_sent, x_landed, y_sent, y_landed, z_sent, z_landed,
 ):
     n = 2 * heads
@@ -252,16 +252,17 @@
     w_copy = remote(w_in, w_full.at[core], w_sent, w_landed, (chip, other))
     w_copy.start()
 
-    def data_copy(head):
+    def data_copy(wave, head):
+        span = pl.ds(2 * wave, 2)
         return remote(
-            x_ref.at[head], full.at[here], sent.at[head], landed.at[here], (base + head, core)
-        )
-
-    def cross_copy(head):
-        lane = pl.ds(pl.multiple_of(core * 2 * HD, 2 * HD), 2 * HD)
+            x_ref.at[head, span], full.at[here, span], sent.at[wave, head],
+            landed.at[wave, here], (base + head, core),
+        )
+
+    def cross_copy(wave, head):
         return remote(
-            x_ref.at[head, :, lane], xfull.at[here], xsent.at[head], xlanded.at[here],
-            (far + head, core),
+            x_ref.at[head, 2 * wave + core], xfull.at[here, wave],
+            xsent.at[wave, head], xlanded.at[wave, here], (far + head, core),
         )
 
     def id_copy(peer):
@@ -286,52 +287,58 @@
 
     per_core = heads // 2
 
-    def prepare(head):
-        x_ref[head, :, 0:HD] = normalize(q_ref[:, lanes(head)])[0].astype(kind)
-        x_ref[head, :, 2 * HD : 3 * HD] = normalize(k_ref[:, lanes(head)])[0].astype(kind)
-        x_ref[head, :, 3 * HD : 4 * HD] = v_ref[:, lanes(head)]
-        w_rows = w_full[head // per_core, lanes(lax.rem(head, per_core)), :]
-        x_ref[head, :, HD : 2 * HD] = dot(c_ref[...], w_rows, 1, 1).astype(kind)
-
-    def send_data(head):
+    def prepare(wave, head):
+        if wave == 0:
+            x_ref[head, 0] = normalize(q_ref[:, lanes(head)])[0].astype(kind)
+            x_ref[head, 1] = normalize(k_ref[:, lanes(head)])[0].astype(kind)
+        else:
+            w_rows = w_full[head // per_core, lanes(lax.rem(head, per_core)), :]
+            x_ref[head, 2] = dot(c_ref[...], w_rows, 1, 1).astype(kind)
+            x_ref[head, 3] = v_ref[:, lanes(head)]
+
+    def send_data(wave, head):
         @pl.when(head != here)
         def _():
-            data_copy(head).start()
-
-    for step, masks in enumerate(order):
-        head = toward(*masks)
-        if step == per_core:
+            data_copy(wave, head).start()
+
+    for wave in range(2):
+        if wave == 1:
             remote(w_in, w_full.at[other], w_sent, w_landed, (chip, other)).wait_recv()
-        prepare(head)
+        for masks in order:
+            head = toward(*masks)
+            prepare(wave, head)
+
+            @pl.when(light)
+            def _(head=head, wave=wave):
+                cross_copy(wave, head).start()
+
+            @pl.when(heavy)
+            def _(head=head, wave=wave):
+                send_data(wave, head)
 
         @pl.when(light)
-        def _(head=head):
-            cross_copy(head).start()
-
-        @pl.when(heavy)
-        def _(head=head):
-            send_data(head)
-
-    @pl.when(light)
-    def _():
-        for masks in order:
-            send_data(toward(*masks))
+        def _(wave=wave):
+            for masks in order:
+                send_data(wave, toward(*masks))
 
     full[here] = x_ref[here]
 
     def wait_ids(peer):
         remote(ids_ref, slots.at[peer], id_sent.at[0], id_landed.at[peer], (chip, other)).wait_recv()
 
-    def pack_one(peer, rows):
+    def mark(peer):
         slot_row = slots[peer]
         down = lax.broadcasted_iota(jnp.int32, (nslots, tokens), 0).astype(jnp.float32)
         hot = jnp.where(down == slot_row[0:1], 1.0, 0.0)
         along = lax.broadcasted_iota(jnp.int32, (tokens, nslots), 1).astype(jnp.float32)
         onehot_t[peer] = jnp.where(along == slot_row.T[:, 0:1], 1.0, 0.0).astype(kind)
+        onehot[peer] = hot.astype(kind)
         valid = jnp.broadcast_to(jnp.sum(hot, axis=1, keepdims=True), (nslots, HD))
-        packed = dot(hot.astype(kind), rows, 1, 0)
-        packed = packed.reshape(clusters, cap, packed.shape[1])
-        return packed, valid.reshape(clusters, cap, HD)
+        return valid.reshape(clusters, cap, HD)
+
+    def pack_one(peer, rows):
+        packed = dot(onehot[peer], rows, 1, 0)
+        return packed.reshape(clusters, cap, packed.shape[1])
 
     def pair_rows(pair):
         return pl.ds(pl.multiple_of(pair * 2 * cap, 2 * cap), 2 * cap)
@@ -341,50 +348,68 @@
         y_bit = lax.rem(step + jnp.where(near_first, 1, 0) * (1 - step // 2), 2)
         return lax.rem(zl + z_bit, 2) * 2 + lax.rem(y + y_bit, 2)
 
-    def pack_own(step, carry):
-        pair = pair_toward(step)
-        parts, valids = [], []
-        for index in range(2):
-            source = 2 * pair + index
-
-            @pl.when(source != here)
-            def _():
-                wait_ids(base + source)
+    def pack_own(wave):
+        span = pl.ds(2 * wave, 2)
+
+        def body(step, carry):
+            pair = pair_toward(step)
+            parts, valids = [], []
+            for index in range(2):
+                source = 2 * pair + index
+
+                @pl.when(source != here)
+                def _():
+                    if wave == 0:
+                        wait_ids(base + source)
+                    remote(
+                        x_ref.at[0, span], full.at[source, span], sent.at[wave, 0],
+                        landed.at[wave, source], (chip, other),
+                    ).wait_recv()
+
+                if wave == 0:
+                    valids.append(mark(base + source))
+                rows = jnp.concatenate(
+                    [full[source, 2 * wave], full[source, 2 * wave + 1]], axis=1
+                )
+                parts.append(pack_one(base + source, rows))
+            both = jnp.concatenate(parts, axis=1).astype(kind)
+            rows = pair_rows(pair)
+            if wave == 0:
+                qk[0, :, rows, :] = both[:, :, 0:HD]
+                qk[1, :, rows, :] = both[:, :, HD:]
+                gv[1, :, rows, HD:] = jnp.concatenate(valids, axis=1).astype(kind)
+            else:
+                gv[0, :, rows, 0:HD] = both[:, :, 0:HD]
+                gv[1, :, rows, 0:HD] = both[:, :, HD:]
+            return carry
+
+        lax.fori_loop(0, pairs, body, 0)
+
+    def pack_cross(wave):
+        def body(step, carry):
+            pair = pair_toward(step)
+            parts, valids = [], []
+            for index in range(2):
+                source = 2 * pair + index
+                if wave == 0:
+                    wait_ids(far + source)
                 remote(
-                    x_ref.at[0], full.at[source], sent.at[0], landed.at[source], (chip, other)
+                    x_ref.at[0, wave], xfull.at[source, wave], xsent.at[wave, 0],
+                    xlanded.at[wave, source], (chip, other),
                 ).wait_recv()
-
-            packed, valid = pack_one(base + source, full[source])
-            parts.append(packed)
-            valids.append(valid)
-        both = jnp.concatenate(parts, axis=1).astype(kind)
-        rows = pair_rows(pair)
-        qk[0, :, rows, :] = both[:, :, 0:HD]
-        gv[0, :, rows, 0:HD] = both[:, :, HD : 2 * HD]
-        qk[1, :, rows, :] = both[:, :, 2 * HD : 3 * HD]
-        gv[1, :, rows, 0:HD] = both[:, :, 3 * HD :]
-        gv[1, :, rows, HD:] = jnp.concatenate(valids, axis=1).astype(kind)
-        return carry
-
-    def pack_cross(step, carry):
-        pair = pair_toward(step)
-        parts, valids = [], []
-        for index in range(2):
-            source = 2 * pair + index
-            wait_ids(far + source)
-            remote(
-                x_ref.at[0, :, 0 : 2 * HD], xfull.at[source], xsent.at[0], xlanded.at[source],
-                (chip, other),
-            ).wait_recv()
-            packed, valid = pack_one(far + source, xfull[source])
-            parts.append(packed)
-            valids.append(valid)
-        both = jnp.concatenate(parts, axis=1).astype(kind)
-        rows = pair_rows(pair)
-        qk[2, :, rows, :] = both[:, :, 0:HD]
-        gv[2, :, rows, 0:HD] = both[:, :, HD:]
-        gv[2, :, rows, HD:] = jnp.concatenate(valids, axis=1).astype(kind)
-        return carry
+                if wave == 0:
+                    valids.append(mark(far + source))
+                parts.append(pack_one(far + source, xfull[source, wave]))
+            both = jnp.concatenate(parts, axis=1).astype(kind)
+            rows = pair_rows(pair)
+            if wave == 0:
+                qk[2, :, rows, :] = both
+                gv[2, :, rows, HD:] = jnp.concatenate(valids, axis=1).astype(kind)
+            else:
+                gv[2, :, rows, 0:HD] = both
+            return carry
+
+        lax.fori_loop(0, pairs, body, 0)
 
     size = 2 * rows_of
     down = lax.broadcasted_iota(jnp.int32, (size, size), 0)
@@ -406,11 +431,21 @@
             2, rows_of, width
         )
 
-    def forward(block, qi, ki, vi, allowed):
-        scores = dot(of(qk, qi, block, 0, HD), of(qk, ki, block, 0, HD), 1, 1)
-        weights = (jnp.exp(scores * inv) * allow_ref[allowed]).astype(kind)
-        both = dot(weights, of(gv, vi, block, 0, 2 * HD), 1, 0)
-        return weights, both[:, :HD], both[:, HD:]
+    def scores(which, qi, ki):
+        def body(step, carry):
+            def one(block):
+                found = dot(of(qk, qi, block, 0, HD), of(qk, ki, block, 0, HD), 1, 1)
+                return block, (jnp.exp(found * inv) * allow_ref[which]).astype(kind)
+
+            for block, weights in each(step, one):
+                e_ref[which, block] = weights
+            return carry
+
+        lax.fori_loop(0, rounds, body, 0)
+
+    def gather(which, block, vi):
+        both = dot(e_ref[which, block], of(gv, vi, block, 0, 2 * HD), 1, 0)
+        return both[:, :HD], both[:, HD:]
 
     def inner(block, grads, top):
         return jnp.sum(
@@ -426,54 +461,49 @@
     def sums(carry, block, total, product):
         return jnp.where(lane == block, total, jnp.where(lane == blocks + block, product, carry))
 
-    cross_rows = other
-    cross_q, cross_k = 2 * other, 1 + core
-    cross_g, cross_v = 2 * other, 1 + core
     shared_rows = heavy.astype(jnp.int32)
+    rounds = blocks // group
+    nothing = jnp.zeros((size, HD), jnp.float32)
 
     def each(step, one):
         return [one(step * group + i) for i in range(group)]
 
     def diagonal_whole(step, carry):
         def one(block):
-            weights, top, total = forward(block, 0, 1, 1, 0)
-            return block, weights, top, total, inner(block, 0, top)
-
-        for block, weights, top, total, product in each(step, one):
-            e_ref[0, block] = weights
+            top, total = gather(0, block, 1)
+            return block, top, total, inner(block, 0, top)
+
+        for block, top, total, product in each(step, one):
             settle(own_out, block, 0, top, total, product)
         return carry
 
     def diagonal_part(step, carry):
         def one(block):
-            weights, top, total = forward(block, 0, 1, 1, 0)
-            return block, weights, top, total, inner(block, 0, top)
-
-        for block, weights, top, total, product in each(step, one):
-            e_ref[0, block] = weights
+            top, total = gather(0, block, 1)
+            return block, top, total, inner(block, 0, top)
+
+        for block, top, total, product in each(step, one):
             num[0, block] = top
-            den[0, block] = total
             carry = sums(carry, block, total, product)
         return carry
 
     def across_keys(step, carry):
         def one(block):
-            weights, top, total = forward(block, 0, 2, 2, 1)
-            top, total = top + num[0, block], total + den[0, block]
-            return block, weights, top, total, inner(block, 0, top)
-
-        for block, weights, top, total, product in each(step, one):
-            e_ref[1, block] = weights
+            top, total = gather(0, block, 1)
+            top_x, total_x = gather(1, block, 2)
+            top, total = top + top_x, total + total_x
+            return block, top, total, inner(block, 0, top)
+
+        for block, top, total, product in each(step, one):
             settle(own_out, block, 0, top, total, product)
         return carry
 
     def across_queries(step, carry):
         def one(block):
-            weights, top, total = forward(block, 2, 1, 1, 1)
-            return block, weights, top, total, inner(block, 2, top)
-
-        for block, weights, top, total, product in each(step, one):
-            e_ref[1, block] = weights
+            top, total = gather(1, block, 1)
+            return block, top, total, inner(block, 2, top)
+
+        for block, top, total, product in each(step, one):
             num[1, block] = top
             carry = sums(carry, block, total, product)
         return carry
@@ -498,52 +528,85 @@
 
         return body
 
-    def backward(block, which, rows, qi, ki, vi, gi):
-        weights = e_ref[which, block]
-        grads = (of(gv, gi, block, 0, HD).astype(jnp.float32) * den[rows, block]).astype(kind)
-        product = dot(grads, of(gv, vi, block, 0, HD), 1, 1)
+    def scaled(block, rows, gi):
+        return (of(gv, gi, block, 0, HD).astype(jnp.float32) * den[rows, block]).astype(kind)
+
+    def value_light(step, carry):
+        for block, found in each(
+            step, lambda block: (block, dot(e_ref[0, block], scaled(block, 0, 0), 0, 0))
+        ):
+            put(own_out, block, 3 * HD, found)
+        return carry
+
+    def value_keys(step, carry):
+        def one(block):
+            grads = scaled(block, 0, 0)
+            return block, dot(e_ref[0, block], grads, 0, 0), dot(e_ref[1, block], grads, 0, 0)
+
+        for block, near, away in each(step, one):
+            put(own_out, block, 3 * HD, near)
+            put(cross_out, block, HD, away)
+        return carry
+
+    def value_queries(step, carry):
+        def one(block):
+            near = dot(e_ref[0, block], scaled(block, 0, 0), 0, 0)
+            return block, near + dot(e_ref[1, block], scaled(block, 1, 2), 0, 0)
+
+        for block, found in each(step, one):
+            put(own_out, block, 3 * HD, found)
+        return carry
+
+    def slopes(block, which, rows, qi, ki, vi, gi):
+        product = dot(scaled(block, rows, gi), of(gv, vi, block, 0, HD), 1, 1)
         delta = num[rows, block]
-        slope = (weights.astype(jnp.float32) * (product - delta)).astype(kind)
+        slope = (e_ref[which, block].astype(jnp.float32) * (product - delta)).astype(kind)
         return (
             dot(slope, of(qk, ki, block, 0, HD), 1, 0) * inv,
             dot(slope, of(qk, qi, block, 0, HD), 0, 0) * inv,
-            dot(weights, grads, 0, 0),
-        )
-
-    def back_light(step, carry):
-        found = [backward(step * group + i, 0, 0, 0, 1, 1, 0) for i in range(group)]
-        for i, grads in enumerate(found):
-            for j in range(3):
-                put(own_out, step * group + i, (j + 1) * HD, grads[j])
-        return carry
-
-    def back_heavy(step, carry):
-        found = []
-        for i in range(group):
-            block = step * group + i
-            found.append(
-                (
-                    backward(block, 0, 0, 0, 1, 1, 0),
-                    backward(block, 1, cross_rows, cross_q, cross_k, cross_v, cross_g),
-                )
-            )
-        share = core.astype(jnp.float32)
-        for i, (near, away) in enumerate(found):
-            block = step * group + i
-            put(own_out, block, HD, near[0] + away[0] * share)
-            put(own_out, block, 2 * HD, near[1] + away[1] * (1.0 - share))
-            put(own_out, block, 3 * HD, near[2] + away[2] * (1.0 - share))
-
-            @pl.when(first)
-            def _(away=away, block=block):
-                put(cross_out, block, HD, away[0])
-
-            @pl.when(jnp.logical_not(first))
-            def _(away=away, block=block):
-                put(cross_out, block, 0, away[1])
-                put(cross_out, block, HD, away[2])
-
-        return carry
+        )
+
+    def slope_light(step, carry):
+        def one(block):
+            return (block,) + slopes(block, 0, 0, 0, 1, 1, 0)
+
+        for block, grad_q, grad_k in each(step, one):
+            put(own_out, block, HD, grad_q)
+            put(own_out, block, 2 * HD, grad_k)
+        return carry
+
+    def slope_keys(step, carry):
+        def one(block):
+            return (block,) + slopes(block, 0, 0, 0, 1, 1, 0) + slopes(block, 1, 0, 0, 2, 2, 0)
+
+        for block, grad_q, grad_k, cross_q, cross_k in each(step, one):
+            put(own_out, block, HD, grad_q + cross_q)
+            put(own_out, block, 2 * HD, grad_k)
+            put(cross_out, block, 0, cross_k)
+        return carry
+
+    def slope_queries(step, carry):
+        def one(block):
+            return (block,) + slopes(block, 0, 0, 0, 1, 1, 0) + slopes(block, 1, 1, 2, 1, 1, 2)
+
+        for block, grad_q, grad_k, cross_q, cross_k in each(step, one):
+            put(own_out, block, HD, grad_q)
+            put(own_out, block, 2 * HD, grad_k + cross_k)
+            put(cross_out, block, HD, cross_q)
+        return carry
+
+    def by_role(for_light, for_queries, for_keys):
+        @pl.when(light)
+        def _():
+            lax.fori_loop(0, rounds, for_light, 0)
+
+        @pl.when(jnp.logical_and(heavy, first))
+        def _():
+            lax.fori_loop(0, rounds, for_queries, 0)
+
+        @pl.when(jnp.logical_and(heavy, jnp.logical_not(first)))
+        def _():
+            lax.fori_loop(0, rounds, for_keys, 0)
 
     def unpack(peer, ref, pair, low, high, index):
         both = ref[:, pair_rows(pair), low:high].astype(jnp.float32)
@@ -552,14 +615,19 @@
 
     def a_copy(head):
         return remote(
-            stage_a.at[head], got_a.at[here], a_sent.at[head], a_landed.at[here],
+            stage_a.at[head, 0], got_a.at[here, 0], a_sent.at[head], a_landed.at[here],
             (base + head, core),
         )
 
     def g_copy(head):
         return remote(
-            stage_g.at[head], got_g.at[here], g_sent.at[head], g_landed.at[here],
-            (base + head, core),
+            stage_g.at[head, pl.ds(0, 2)], got_g.at[here, pl.ds(0, 2)], g_sent.at[head],
+            g_landed.at[here], (base + head, core),
+        )
+
+    def v_copy(head):
+        return remote(
+            stage_g.at[head, 2], got_g.at[here, 2], v_sent.at[head], v_landed.at[here], (base + head, core),
         )
 
     def cx_copy(index, head):
@@ -568,12 +636,14 @@
             cx_landed.at[index, here], (far + head, core),
         )
 
-    def return_own(low, high, stage, got, copy):
+    def return_own(low, high, stage, got, at, copy):
         def body(step, carry):
             pair = pair_toward(step)
             for index in range(2):
                 target = 2 * pair + index
-                stage[target] = unpack(base + target, own_out, pair, low, high, index)
+                found = unpack(base + target, own_out, pair, low, high, index)
+                for part in range((high - low) // HD):
+                    stage[target, at + part] = found[:, part * HD : (part + 1) * HD]
 
                 @pl.when(target != here)
                 def _():
@@ -581,7 +651,8 @@
 
                 @pl.when(target == here)
                 def _():
-                    got[target] = stage[target]
+                    for part in range((high - low) // HD):
+                        got[target, at + part] = stage[target, at + part]
 
             return carry
 
@@ -600,61 +671,60 @@
 
         lax.fori_loop(0, pairs, body, 0)
 
-    rounds = blocks // group
-    nothing = jnp.zeros((size, HD), jnp.float32)
-    lax.fori_loop(0, pairs, pack_own, 0)
-
-    @pl.when(heavy == first)
-    def _():
-        lax.fori_loop(0, rounds, diagonal_whole, 0)
-
-    @pl.when(heavy != first)
-    def _():
-        st_mine[...] = lax.fori_loop(0, rounds, diagonal_part, nothing)
+    pack_own(0)
+    scores(0, 0, 1)
 
     @pl.when(heavy)
     def _():
-        lax.fori_loop(0, pairs, pack_cross, 0)
-
-        @pl.when(jnp.logical_not(first))
-        def _():
-            lax.fori_loop(0, rounds, across_keys, 0)
-
-        @pl.when(first)
-        def _():
-            st_mine[...] = lax.fori_loop(0, rounds, across_queries, nothing)
+        pack_cross(0)
+        scores(1, 2 * other, 1 + core)
+
+    @pl.when(heavy)
+    def _():
+        pack_cross(1)
+
+    pack_own(1)
 
     @pl.when(first)
     def _():
-        st_copy().start()
-        st_copy().wait_recv()
-
         @pl.when(heavy)
         def _():
+            st_mine[...] = lax.fori_loop(0, rounds, across_queries, nothing)
+            st_copy().start()
+            lax.fori_loop(0, rounds, diagonal_whole, 0)
+            return_own(0, HD, stage_a, got_a, 0, a_copy)
+            st_copy().wait_recv()
             lax.fori_loop(0, rounds, settle_shared(cross_out), 0)
             return_cross(0)
 
         @pl.when(light)
         def _():
+            st_mine[...] = lax.fori_loop(0, rounds, diagonal_part, nothing)
+            st_copy().start()
+            st_copy().wait_recv()
             lax.fori_loop(0, rounds, settle_shared(own_out), 0)
 
-    return_own(0, HD, stage_a, got_a, a_copy)
-
-    @pl.when(light)
+    @pl.when(jnp.logical_not(first))
     def _():
-        lax.fori_loop(0, blocks // group, back_light, 0)
-
-    @pl.when(heavy)
+        @pl.when(heavy)
+        def _():
+            lax.fori_loop(0, rounds, across_keys, 0)
+
+        @pl.when(light)
+        def _():
+            lax.fori_loop(0, rounds, diagonal_whole, 0)
+
+    @pl.when(jnp.logical_not(jnp.logical_and(first, heavy)))
     def _():
-        lax.fori_loop(0, blocks // group, back_heavy, 0)
-
-        @pl.when(jnp.logical_not(first))
-        def _():
-            return_cross(0)
-
+        return_own(0, HD, stage_a, got_a, 0, a_copy)
+
+    by_role(value_light, value_queries, value_keys)
+
+    @pl.when(jnp.logical_and(heavy, jnp.logical_not(first)))
+    def _():
         return_cross(1)
 
-    return_own(HD, 4 * HD, stage_g, got_g, g_copy)
+    return_own(3 * HD, 4 * HD, stage_g, got_g, 2, v_copy)
 
     piece = w_ref.shape[2]
 
@@ -701,19 +771,19 @@
         @pl.when(head != here)
         def _():
             remote(
-                stage_a.at[0], got_a.at[head], a_sent.at[0], a_landed.at[head], (chip, other)
+                stage_a.at[0, 0], got_a.at[head, 0], a_sent.at[0], a_landed.at[head], (chip, other)
             ).wait_recv()
 
         @pl.when(jnp.logical_and(first, light))
         def _():
             wait_cross(0, head)
             a_ref[:, lanes(head)] = (
-                got_a[head].astype(jnp.float32) + got_x[0, head].astype(jnp.float32)
+                got_a[head, 0].astype(jnp.float32) + got_x[0, head].astype(jnp.float32)
             ).astype(kind)
 
         @pl.when(jnp.logical_not(jnp.logical_and(first, light)))
         def _():
-            a_ref[:, lanes(head)] = got_a[head]
+            a_ref[:, lanes(head)] = got_a[head, 0]
 
         total = dot(a_ref[:, lanes(head)], c_ref[...], 0, 0)
         for index in range(4):
@@ -778,6 +848,19 @@
 
     lax.fori_loop(0, heads, term, 0)
     lax.fori_loop(0, n // 2, x_phase, 0)
+    by_role(slope_light, slope_queries, slope_keys)
+
+    @pl.when(jnp.logical_and(heavy, first))
+    def _():
+        return_cross(1)
+
+    @pl.when(jnp.logical_and(heavy, jnp.logical_not(first)))
+    def _():
+        return_cross(0)
+
+    return_own(HD, 3 * HD, stage_g, got_g, 0, g_copy)
+    lax.fori_loop(0, quarter, y_phase, 0)
+    lax.fori_loop(0, quarter, z_phase, 0)
 
     depth = w_full.shape[1]
     tile = 2 * HD
@@ -793,7 +876,6 @@
     lax.fori_loop(0, out_ref.shape[1] // tile, project, 0)
     keep_out = pltpu.make_async_copy(out_ref, out_out, stored.at[0])
     keep_out.start()
-    lax.fori_loop(0, quarter, y_phase, 0)
 
     results = ((gq_ref, gq_out), (gk_ref, gk_out), (gv_ref, gv_out))
 
@@ -808,11 +890,15 @@
 
         @pl.when(head != here)
         def _():
-            remote(
-                stage_g.at[0], got_g.at[head], g_sent.at[0], g_landed.at[head], (chip, other)
-            ).wait_recv()
-
-        grads = [got_g[head, :, i * HD : (i + 1) * HD].astype(jnp.float32) for i in range(3)]
+            for span, gone, come in (
+                (pl.ds(2, 1), v_sent, v_landed), (pl.ds(0, 2), g_sent, g_landed)
+            ):
+                remote(
+                    stage_g.at[0, span], got_g.at[head, span], gone.at[0], come.at[head],
+                    (chip, other),
+                ).wait_recv()
+
+        grads = [got_g[head, i].astype(jnp.float32) for i in range(3)]
 
         @pl.when(light)
         def _():
@@ -837,7 +923,6 @@
             keep(index, head).start()
         return carry
 
-    lax.fori_loop(0, quarter, z_phase, 0)
     lax.fori_loop(0, heads, finish, 0)
     lax.fori_loop(0, quarter, z_sum, 0)
     grad_ref[...] = grad_ref[...] * scale
@@ -852,14 +937,17 @@
         @pl.when(head != here)
         def _():
             id_copy(base + head).wait_send()
-            data_copy(head).wait_send()
+            data_copy(0, head).wait_send()
+            data_copy(1, head).wait_send()
             a_copy(head).wait_send()
             g_copy(head).wait_send()
+            v_copy(head).wait_send()
 
         @pl.when(light)
         def _():
             id_copy(far + head).wait_send()
-            cross_copy(head).wait_send()
+            cross_copy(0, head).wait_send()
+            cross_copy(1, head).wait_send()
 
         @pl.when(heavy)
         def _():
@@ -895,12 +983,13 @@
         (c.shape, kind), (piece, wide),
         (q.shape, kind), (q.shape, kind), (q.shape, kind), (c.shape, kind),
         ((2,) + w.shape, kind),
-        ((heads, tokens, 4 * HD), kind),
-        ((heads, tokens, 4 * HD), kind),
-        ((heads, tokens, 2 * HD), kind),
+        ((heads, 4, tokens, HD), kind),
+        ((heads, 4, tokens, HD), kind),
+        ((heads, 2, tokens, HD), kind),
         ((8, tokens), wide),
         ((n, 8, tokens), wide),
         ((n, tokens, nslots), kind),
+        ((n, nslots, tokens), kind),
         ((2, pair, pair), wide),
         ((3, clusters, rows, HD), kind),
         ((3, clusters, rows, 2 * HD), kind),
@@ -911,11 +1000,11 @@
         ((clusters, rows, 2 * HD), kind),
         ((pair, HD), wide),
         ((pair, HD), wide),
-        ((heads, tokens, HD), kind),
-        ((heads, tokens, 3 * HD), kind),
+        ((heads, 1, tokens, HD), kind),
+        ((heads, 3, tokens, HD), kind),
         ((2, heads, tokens, HD), kind),
-        ((heads, tokens, HD), kind),
-        ((heads, tokens, 3 * HD), kind),
+        ((heads, 1, tokens, HD), kind),
+        ((heads, 3, tokens, HD), kind),
         ((2, heads, tokens, HD), kind),
         (q.shape, kind),
         ((n, 2) + piece, kind),
@@ -930,9 +1019,9 @@
         return pltpu.SemaphoreType.DMA(count)
 
     semaphores = (
-        [many(2), many(3, heads), many(5), one, one, many(heads), many(heads), many(heads), many(heads), many(n), many(n)]
+        [many(2), many(3, heads), many(5), one, one] + [many(2, heads)] * 4 + [many(n)] * 2
         + [one, one]
-        + [many(heads)] * 4
+        + [many(heads)] * 6
         + [many(2, heads)] * 2
         + [many(n)] * 2
         + [many(n // 2)] * 2

time: 117 us -> 104 us (0.89)
  Pallas kernels: 115 us -> 102 us
    pallas_call x1, Pallas kernels: 112 us -> 99.8 us  [layer_call(): pl.pallas_call(functools.partial(layer_kernel, heads, scale), out_shape=(...]
where the time goes in v3:
time: 104 us; the launch traced here: 103 us
  Pallas kernels  102 us (98%)
    pallas_call x1, Pallas kernels, layer_call(): pl.pallas_call(functools.partial(layer_kernel, heads, scale), out_shape=(...  99.8 us
    pallas_call x1, Pallas kernels, hand_over(): pl.pallas_call(functools.partial(hand_over_kernel, count), out_shape=tupl...  2.47 us

profile of v3, /device:TPU:0, one launch (start us, length us, event | category | flops | bytes accessed | tf_op | source)
XLA Modules:
  0.0 102.9 jit_solution(4570997419042547857)
XLA Ops:
  0.6 99.8 %shard_map.101 = (bf16[256,1024]{1,0:T(8,128)(2,1)}, bf16[256,1024]{1,0:T(8,128)(2,1)}, bf16[256,1024]{1,0:T(8,128)(2,1)}, bf16[256,1024]{1,0:T(8,128)(2,1)}, f32[32,1024]{1,0:T(8,128)}) custom-call(bf16[256,1024]{1,0:T(8,128)(2,1)} %bitcast.8, bf16[256,1024]{1,0:T(8,128)(2,1)} %bitcast.9, bf16[256,1024]{1,0:T(8,128)(2,1)} %bitcast.10, ...), custom_call_target="tpu_custom_call" | custom-call | tf_op jit(solution)/shard_map/pallas_call | solution.py:1030
  100.5 2.5 %shard_map.102 = (bf16[256,1024]{1,0:T(8,128)(2,1)}, bf16[256,1024]{1,0:T(8,128)(2,1)}, bf16[256,1024]{1,0:T(8,128)(2,1)}, bf16[256,1024]{1,0:T(8,128)(2,1)}, f32[32,1024]{1,0:T(8,128)}) custom-call(bf16[256,1024]{1,0:T(8,128)(2,1)} %get-tuple-element.15.refs_0_, bf16[256,1024]{1,0:T(8,128)(2,1)} %get-tuple-element.16.refs_1_, ...), custom_call_target="tpu_custom_call" | custom-call | tf_op jit(solution)/shard_map/pallas_call | solution.py:1062

commit v4 on v3

--- a/solution.py
+++ b/solution.py
@@ -252,16 +252,19 @@
     w_copy = remote(w_in, w_full.at[core], w_sent, w_landed, (chip, other))
     w_copy.start()
 
+    spans = (pl.ds(0, 2), pl.ds(2, 1), pl.ds(3, 1))
+
     def data_copy(wave, head):
-        span = pl.ds(2 * wave, 2)
+        span = spans[wave]
         return remote(
             x_ref.at[head, span], full.at[here, span], sent.at[wave, head],
             landed.at[wave, here], (base + head, core),
         )
 
     def cross_copy(wave, head):
+        row = core if wave == 0 else 3 - core
         return remote(
-            x_ref.at[head, 2 * wave + core], xfull.at[here, wave],
+            x_ref.at[head, row], xfull.at[here, wave],
             xsent.at[wave, head], xlanded.at[wave, here], (far + head, core),
         )
 
@@ -291,26 +294,28 @@
         if wave == 0:
             x_ref[head, 0] = normalize(q_ref[:, lanes(head)])[0].astype(kind)
             x_ref[head, 1] = normalize(k_ref[:, lanes(head)])[0].astype(kind)
+        elif wave == 1:
+            x_ref[head, 2] = v_ref[:, lanes(head)]
         else:
             w_rows = w_full[head // per_core, lanes(lax.rem(head, per_core)), :]
-            x_ref[head, 2] = dot(c_ref[...], w_rows, 1, 1).astype(kind)
-            x_ref[head, 3] = v_ref[:, lanes(head)]
+            x_ref[head, 3] = dot(c_ref[...], w_rows, 1, 1).astype(kind)
 
     def send_data(wave, head):
         @pl.when(head != here)
         def _():
             data_copy(wave, head).start()
 
-    for wave in range(2):
-        if wave == 1:
+    for wave in range(3):
+        if wave == 2:
             remote(w_in, w_full.at[other], w_sent, w_landed, (chip, other)).wait_recv()
+        to_cross = (light, jnp.logical_and(light, other == 0), jnp.logical_and(light, first))[wave]
         for masks in order:
             head = toward(*masks)
             prepare(wave, head)
 
-            @pl.when(light)
+            @pl.when(to_cross)
             def _(head=head, wave=wave):
-                cross_copy(wave, head).start()
+                cross_copy(min(wave, 1), head).start()
 
             @pl.when(heavy)
             def _(head=head, wave=wave):
@@ -349,7 +354,7 @@
         return lax.rem(zl + z_bit, 2) * 2 + lax.rem(y + y_bit, 2)
 
     def pack_own(wave):
-        span = pl.ds(2 * wave, 2)
+        span = spans[wave]
 
         def body(step, carry):
             pair = pair_toward(step)
@@ -368,9 +373,10 @@
 
                 if wave == 0:
                     valids.append(mark(base + source))
-                rows = jnp.concatenate(
-                    [full[source, 2 * wave], full[source, 2 * wave + 1]], axis=1
-                )
+                if wave == 0:
+                    rows = jnp.concatenate([full[source, 0], full[source, 1]], axis=1)
+                else:
+                    rows = full[source, wave + 1]
                 parts.append(pack_one(base + source, rows))
             both = jnp.concatenate(parts, axis=1).astype(kind)
             rows = pair_rows(pair)
@@ -379,8 +385,7 @@
                 qk[1, :, rows, :] = both[:, :, HD:]
                 gv[1, :, rows, HD:] = jnp.concatenate(valids, axis=1).astype(kind)
             else:
-                gv[0, :, rows, 0:HD] = both[:, :, 0:HD]
-                gv[1, :, rows, 0:HD] = both[:, :, HD:]
+                gv[2 - wave, :, rows, 0:HD] = both
             return carry
 
         lax.fori_loop(0, pairs, body, 0)
@@ -415,7 +420,7 @@
     down = lax.broadcasted_iota(jnp.int32, (size, size), 0)
     along = lax.broadcasted_iota(jnp.int32, (size, size), 1)
     lane = lax.broadcasted_iota(jnp.int32, (size, HD), 1)
-    group = 4
+    group = 8
 
     one_cluster = (down < rows_of) == (along < rows_of)
     allow_ref[0] = jnp.where(jnp.logical_and(one_cluster, along <= down), 1.0, 0.0)
@@ -452,14 +457,13 @@
             of(gv, grads, block, 0, HD).astype(jnp.float32) * top, axis=1, keepdims=True
         )
 
-    def settle(target, block, rows, top, total, product):
+    def settle(target, block, rows, top, total):
         factor = 1.0 / jnp.where(total > 0, total, 1.0)
         den[rows, block] = jnp.broadcast_to(factor, (size, HD))
-        num[rows, block] = jnp.broadcast_to(product * (factor * factor), (size, HD))
         put(target, block, 0, top * factor)
 
-    def sums(carry, block, total, product):
-        return jnp.where(lane == block, total, jnp.where(lane == blocks + block, product, carry))
+    def pick(found, block):
+        return jnp.sum(jnp.where(lane == block, found, 0.0), axis=1, keepdims=True)
 
     shared_rows = heavy.astype(jnp.int32)
     rounds = blocks // group
@@ -469,64 +473,60 @@
         return [one(step * group + i) for i in range(group)]
 
     def diagonal_whole(step, carry):
-        def one(block):
-            top, total = gather(0, block, 1)
-            return block, top, total, inner(block, 0, top)
-
-        for block, top, total, product in each(step, one):
-            settle(own_out, block, 0, top, total, product)
+        for block, top, total in each(step, lambda block: (block,) + gather(0, block, 1)):
+            num[0, block] = top
+            settle(own_out, block, 0, top, total)
         return carry
 
     def diagonal_part(step, carry):
-        def one(block):
-            top, total = gather(0, block, 1)
-            return block, top, total, inner(block, 0, top)
-
-        for block, top, total, product in each(step, one):
+        for block, top, total in each(step, lambda block: (block,) + gather(0, block, 1)):
             num[0, block] = top
-            carry = sums(carry, block, total, product)
+            carry = jnp.where(lane == block, total, carry)
         return carry
 
     def across_keys(step, carry):
         def one(block):
             top, total = gather(0, block, 1)
             top_x, total_x = gather(1, block, 2)
-            top, total = top + top_x, total + total_x
-            return block, top, total, inner(block, 0, top)
-
-        for block, top, total, product in each(step, one):
-            settle(own_out, block, 0, top, total, product)
+            return block, top + top_x, total + total_x
+
+        for block, top, total in each(step, one):
+            num[0, block] = top
+            settle(own_out, block, 0, top, total)
         return carry
 
     def across_queries(step, carry):
-        def one(block):
-            top, total = gather(1, block, 1)
-            return block, top, total, inner(block, 2, top)
-
-        for block, top, total, product in each(step, one):
+        for block, top, total in each(step, lambda block: (block,) + gather(1, block, 1)):
             num[1, block] = top
-            carry = sums(carry, block, total, product)
-        return carry
-
-    def st_copy():
-        return remote(st_mine, st_got, st_sent, st_landed, (far + here, core))
+            carry = jnp.where(lane == block, total, carry)
+        return carry
+
+    def st_copy(index):
+        return remote(
+            st_mine.at[index], st_got.at[index], st_sent.at[index], st_landed.at[index],
+            (far + here, core),
+        )
 
     def settle_shared(target):
         def body(step, carry):
-            both = st_mine[...] + st_got[...]
+            both = st_mine[0] + st_got[0]
 
             def one(block):
-                total = jnp.sum(jnp.where(lane == block, both, 0.0), axis=1, keepdims=True)
-                product = jnp.sum(
-                    jnp.where(lane == blocks + block, both, 0.0), axis=1, keepdims=True
-                )
-                return block, num[shared_rows, block], total, product
-
-            for block, top, total, product in each(step, one):
-                settle(target, block, shared_rows, top, total, product)
+                return block, num[shared_rows, block], pick(both, block)
+
+            for block, top, total in each(step, one):
+                settle(target, block, shared_rows, top, total)
             return carry
 
         return body
+
+    def shared_inner(step, carry):
+        def one(block):
+            return block, inner(block, 2 * shared_rows, num[shared_rows, block])
+
+        for block, product in each(step, one):
+            carry = jnp.where(lane == block, product, carry)
+        return carry
 
     def scaled(block, rows, gi):
         return (of(gv, gi, block, 0, HD).astype(jnp.float32) * den[rows, block]).astype(kind)
@@ -557,23 +557,31 @@
             put(own_out, block, 3 * HD, found)
         return carry
 
-    def slopes(block, which, rows, qi, ki, vi, gi):
+    def slopes(block, which, rows, qi, ki, vi, gi, shared=False):
         product = dot(scaled(block, rows, gi), of(gv, vi, block, 0, HD), 1, 1)
-        delta = num[rows, block]
+        if shared:
+            total = pick(st_mine[1] + st_got[1], block)
+        else:
+            total = inner(block, gi, num[rows, block])
+        factor = den[rows, block]
+        delta = total * factor * factor
         slope = (e_ref[which, block].astype(jnp.float32) * (product - delta)).astype(kind)
         return (
             dot(slope, of(qk, ki, block, 0, HD), 1, 0) * inv,
             dot(slope, of(qk, qi, block, 0, HD), 0, 0) * inv,
         )
 
-    def slope_light(step, carry):
-        def one(block):
-            return (block,) + slopes(block, 0, 0, 0, 1, 1, 0)
-
-        for block, grad_q, grad_k in each(step, one):
-            put(own_out, block, HD, grad_q)
-            put(own_out, block, 2 * HD, grad_k)
-        return carry
+    def slope_light(shared):
+        def body(step, carry):
+            def one(block):
+                return (block,) + slopes(block, 0, 0, 0, 1, 1, 0, shared)
+
+            for block, grad_q, grad_k in each(step, one):
+                put(own_out, block, HD, grad_q)
+                put(own_out, block, 2 * HD, grad_k)
+            return carry
+
+        return body
 
     def slope_keys(step, carry):
         def one(block):
@@ -587,7 +595,8 @@
 
     def slope_queries(step, carry):
         def one(block):
-            return (block,) + slopes(block, 0, 0, 0, 1, 1, 0) + slopes(block, 1, 1, 2, 1, 1, 2)
+            near = slopes(block, 0, 0, 0, 1, 1, 0)
+            return (block,) + near + slopes(block, 1, 1, 2, 1, 1, 2, True)
 
         for block, grad_q, grad_k, cross_q, cross_k in each(step, one):
             put(own_out, block, HD, grad_q)
@@ -595,18 +604,14 @@
             put(cross_out, block, HD, cross_q)
         return carry
 
-    def by_role(for_light, for_queries, for_keys):
-        @pl.when(light)
-        def _():
-            lax.fori_loop(0, rounds, for_light, 0)
-
-        @pl.when(jnp.logical_and(heavy, first))
-        def _():
-            lax.fori_loop(0, rounds, for_queries, 0)
-
-        @pl.when(jnp.logical_and(heavy, jnp.logical_not(first)))
-        def _():
-            lax.fori_loop(0, rounds, for_keys, 0)
+    def by_role(light_queries, light_keys, heavy_queries, heavy_keys):
+        for role, sequence, body in (
+            (light, first, light_queries), (light, other == 0, light_keys),
+            (heavy, first, heavy_queries), (heavy, other == 0, heavy_keys),
+        ):
+            @pl.when(jnp.logical_and(role, sequence))
+            def _(body=body):
+                lax.fori_loop(0, rounds, body, 0)
 
     def unpack(peer, ref, pair, low, high, index):
         both = ref[:, pair_rows(pair), low:high].astype(jnp.float32)
@@ -679,32 +684,37 @@
         pack_cross(0)
         scores(1, 2 * other, 1 + core)
 
-    @pl.when(heavy)
+    @pl.when(jnp.logical_and(heavy, other == 0))
     def _():
         pack_cross(1)
 
     pack_own(1)
+
+    def return_attn():
+        return_own(0, HD, stage_a, got_a, 0, a_copy)
 
     @pl.when(first)
     def _():
         @pl.when(heavy)
         def _():
-            st_mine[...] = lax.fori_loop(0, rounds, across_queries, nothing)
-            st_copy().start()
+            st_mine[0] = lax.fori_loop(0, rounds, across_queries, nothing)
+            st_copy(0).start()
             lax.fori_loop(0, rounds, diagonal_whole, 0)
-            return_own(0, HD, stage_a, got_a, 0, a_copy)
-            st_copy().wait_recv()
+            return_attn()
+            st_copy(0).wait_recv()
             lax.fori_loop(0, rounds, settle_shared(cross_out), 0)
             return_cross(0)
+            pack_cross(1)
 
         @pl.when(light)
         def _():
-            st_mine[...] = lax.fori_loop(0, rounds, diagonal_part, nothing)
-            st_copy().start()
-            st_copy().wait_recv()
+            st_mine[0] = lax.fori_loop(0, rounds, diagonal_part, nothing)
+            st_copy(0).start()
+            st_copy(0).wait_recv()
             lax.fori_loop(0, rounds, settle_shared(own_out), 0)
-
-    @pl.when(jnp.logical_not(first))
+            return_attn()
+
+    @pl.when(other == 0)
     def _():
         @pl.when(heavy)
         def _():
@@ -714,11 +724,16 @@
         def _():
             lax.fori_loop(0, rounds, diagonal_whole, 0)
 
-    @pl.when(jnp.logical_not(jnp.logical_and(first, heavy)))
+        return_attn()
+
+    pack_own(2)
+
+    @pl.when(first)
     def _():
-        return_own(0, HD, stage_a, got_a, 0, a_copy)
-
-    by_role(value_light, value_queries, value_keys)
+        st_mine[1] = lax.fori_loop(0, rounds, shared_inner, nothing)
+        st_copy(1).start()
+
+    by_role(value_light, value_light, value_queries, value_keys)
 
     @pl.when(jnp.logical_and(heavy, jnp.logical_not(first)))
     def _():
@@ -848,7 +863,12 @@
 
     lax.fori_loop(0, heads, term, 0)
     lax.fori_loop(0, n // 2, x_phase, 0)
-    by_role(slope_light, slope_queries, slope_keys)
+
+    @pl.when(first)
+    def _():
+        st_copy(1).wait_recv()
+
+    by_role(slope_light(True), slope_light(False), slope_queries, slope_keys)
 
     @pl.when(jnp.logical_and(heavy, first))
     def _():
@@ -939,6 +959,7 @@
             id_copy(base + head).wait_send()
             data_copy(0, head).wait_send()
             data_copy(1, head).wait_send()
+            data_copy(2, head).wait_send()
             a_copy(head).wait_send()
             g_copy(head).wait_send()
             v_copy(head).wait_send()
@@ -963,7 +984,8 @@
 
     @pl.when(first)
     def _():
-        st_copy().wait_send()
+        st_copy(0).wait_send()
+        st_copy(1).wait_send()
 
 
 def layer_call(q, k, v, c, w, labels, clusters, scale):
@@ -998,8 +1020,8 @@
         ((2, blocks, pair, HD), wide),
         ((clusters, rows, 4 * HD), kind),
         ((clusters, rows, 2 * HD), kind),
-        ((pair, HD), wide),
-        ((pair, HD), wide),
+        ((2, pair, HD), wide),
+        ((2, pair, HD), wide),
         ((heads, 1, tokens, HD), kind),
         ((heads, 3, tokens, HD), kind),
         ((2, heads, tokens, HD), kind),
@@ -1019,8 +1041,11 @@
         return pltpu.SemaphoreType.DMA(count)
 
     semaphores = (
-        [many(2), many(3, heads), many(5), one, one] + [many(2, heads)] * 4 + [many(n)] * 2
-        + [one, one]
+        [many(2), many(3, heads), many(5), one, one]
+        + [many(3, heads)] * 2
+        + [many(2, heads)] * 2
+        + [many(n)] * 2
+        + [many(2)] * 2
         + [many(heads)] * 6
         + [many(2, heads)] * 2
         + [many(n)] * 2

time: 104 us -> 98.2 us (0.944)
  Pallas kernels: 102 us -> 96.1 us
    pallas_call x1, Pallas kernels: 99.8 us -> 93.6 us  [layer_call(): pl.pallas_call(functools.partial(layer_kernel, heads, scale), out_shape=(...]
where the time goes in v4:
time: 98.2 us; the launch traced here: 96.9 us
  Pallas kernels  96.1 us (98%)
    pallas_call x1, Pallas kernels, layer_call(): pl.pallas_call(functools.partial(layer_kernel, heads, scale), out_shape=(...  93.6 us
    pallas_call x1, Pallas kernels, hand_over(): pl.pallas_call(functools.partial(hand_over_kernel, count), out_shape=tupl...  2.47 us

profile of v4, /device:TPU:0, one launch (start us, length us, event | category | flops | bytes accessed | tf_op | source)
XLA Modules:
  0.0 96.9 jit_solution(6133301728504163548)
XLA Ops:
  0.6 93.6 %shard_map.101 = (bf16[256,1024]{1,0:T(8,128)(2,1)}, bf16[256,1024]{1,0:T(8,128)(2,1)}, bf16[256,1024]{1,0:T(8,128)(2,1)}, bf16[256,1024]{1,0:T(8,128)(2,1)}, f32[32,1024]{1,0:T(8,128)}) custom-call(bf16[256,1024]{1,0:T(8,128)(2,1)} %bitcast.8, bf16[256,1024]{1,0:T(8,128)(2,1)} %bitcast.9, bf16[256,1024]{1,0:T(8,128)(2,1)} %bitcast.10, ...), custom_call_target="tpu_custom_call" | custom-call | tf_op jit(solution)/shard_map/pallas_call | solution.py:1055
  94.2 2.5 %shard_map.102 = (bf16[256,1024]{1,0:T(8,128)(2,1)}, bf16[256,1024]{1,0:T(8,128)(2,1)}, bf16[256,1024]{1,0:T(8,128)(2,1)}, bf16[256,1024]{1,0:T(8,128)(2,1)}, f32[32,1024]{1,0:T(8,128)}) custom-call(bf16[256,1024]{1,0:T(8,128)(2,1)} %get-tuple-element.15.refs_0_, bf16[256,1024]{1,0:T(8,128)(2,1)} %get-tuple-element.16.refs_1_, ...), custom_call_target="tpu_custom_call" | custom-call | tf_op jit(solution)/shard_map/pallas_call | solution.py:1087

commit v5 on v4

--- a/solution.py
+++ b/solution.py
@@ -285,7 +285,7 @@
         return carry
 
     lax.fori_loop(0, heads, send_ids, 0)
-    for load in loads:
+    for load in loads[:2]:
         load.wait()
 
     per_core = heads // 2
@@ -306,6 +306,9 @@
             data_copy(wave, head).start()
 
     for wave in range(3):
+        if wave == 1:
+            for load in loads[2:]:
+                load.wait()
         if wave == 2:
             remote(w_in, w_full.at[other], w_sent, w_landed, (chip, other)).wait_recv()
         to_cross = (light, jnp.logical_and(light, other == 0), jnp.logical_and(light, first))[wave]
@@ -420,7 +423,7 @@
     down = lax.broadcasted_iota(jnp.int32, (size, size), 0)
     along = lax.broadcasted_iota(jnp.int32, (size, size), 1)
     lane = lax.broadcasted_iota(jnp.int32, (size, HD), 1)
-    group = 8
+    group = 16
 
     one_cluster = (down < rows_of) == (along < rows_of)
     allow_ref[0] = jnp.where(jnp.logical_and(one_cluster, along <= down), 1.0, 0.0)
@@ -661,7 +664,7 @@
 
             return carry
 
-        lax.fori_loop(0, pairs, body, 0)
+        lax.fori_loop(0, pairs, body, 0, unroll=True)
 
     def return_cross(part):
         def body(step, carry):
@@ -674,7 +677,7 @@
                 cx_copy(part, target).start()
             return carry
 
-        lax.fori_loop(0, pairs, body, 0)
+        lax.fori_loop(0, pairs, body, 0, unroll=True)
 
     pack_own(0)
     scores(0, 0, 1)

time: 98.2 us -> 97.4 us (level)
  no operation moved by 1% of the time
where the time goes in v5:
time: 97.4 us; the launch traced here: 96.6 us
  Pallas kernels  95.8 us (98%)
    pallas_call x1, Pallas kernels, layer_call(): pl.pallas_call(functools.partial(layer_kernel, heads, scale), out_shape=(...  93.3 us
    pallas_call x1, Pallas kernels, hand_over(): pl.pallas_call(functools.partial(hand_over_kernel, count), out_shape=tupl...  2.47 us

profile of v5, /device:TPU:0, one launch (start us, length us, event | category | flops | bytes accessed | tf_op | source)
XLA Modules:
  0.0 96.6 jit_solution(3808737784661072661)
XLA Ops:
  0.6 93.3 %shard_map.101 = (bf16[256,1024]{1,0:T(8,128)(2,1)}, bf16[256,1024]{1,0:T(8,128)(2,1)}, bf16[256,1024]{1,0:T(8,128)(2,1)}, bf16[256,1024]{1,0:T(8,128)(2,1)}, f32[32,1024]{1,0:T(8,128)}) custom-call(bf16[256,1024]{1,0:T(8,128)(2,1)} %bitcast.8, bf16[256,1024]{1,0:T(8,128)(2,1)} %bitcast.9, bf16[256,1024]{1,0:T(8,128)(2,1)} %bitcast.10, ...), custom_call_target="tpu_custom_call" | custom-call | tf_op jit(solution)/shard_map/pallas_call | solution.py:1058
  93.9 2.5 %shard_map.102 = (bf16[256,1024]{1,0:T(8,128)(2,1)}, bf16[256,1024]{1,0:T(8,128)(2,1)}, bf16[256,1024]{1,0:T(8,128)(2,1)}, bf16[256,1024]{1,0:T(8,128)(2,1)}, f32[32,1024]{1,0:T(8,128)}) custom-call(bf16[256,1024]{1,0:T(8,128)(2,1)} %get-tuple-element.15.refs_0_, bf16[256,1024]{1,0:T(8,128)(2,1)} %get-tuple-element.16.refs_1_, ...), custom_call_target="tpu_custom_call" | custom-call | tf_op jit(solution)/shard_map/pallas_call | solution.py:1090

commit v6 on v5

--- a/solution.py
+++ b/solution.py
@@ -864,8 +864,8 @@
         w_swap(2 * j + 1).wait_send()
         return carry
 
-    lax.fori_loop(0, heads, term, 0)
-    lax.fori_loop(0, n // 2, x_phase, 0)
+    lax.fori_loop(0, heads, term, 0, unroll=2)
+    lax.fori_loop(0, n // 2, x_phase, 0, unroll=4)
 
     @pl.when(first)
     def _():
@@ -896,7 +896,7 @@
         out_ref[:, columns] = total.astype(out_ref.dtype)
         return carry
 
-    lax.fori_loop(0, out_ref.shape[1] // tile, project, 0)
+    lax.fori_loop(0, out_ref.shape[1] // tile, project, 0, unroll=True)
     keep_out = pltpu.make_async_copy(out_ref, out_out, stored.at[0])
     keep_out.start()
 
@@ -946,7 +946,7 @@
             keep(index, head).start()
         return carry
 
-    lax.fori_loop(0, heads, finish, 0)
+    lax.fori_loop(0, heads, finish, 0, unroll=2)
     lax.fori_loop(0, quarter, z_sum, 0)
     grad_ref[...] = grad_ref[...] * scale
     keep_grad = pltpu.make_async_copy(grad_ref, grad_out, stored.at[1])

time: 97.4 us -> 97.2 us (level)
  no operation moved by 1% of the time
where the time goes in v6:
time: 97.2 us; the launch traced here: 96.6 us
  Pallas kernels  95.8 us (99%)
    pallas_call x1, Pallas kernels, layer_call(): pl.pallas_call(functools.partial(layer_kernel, heads, scale), out_shape=(...  93.3 us
    pallas_call x1, Pallas kernels, hand_over(): pl.pallas_call(functools.partial(hand_over_kernel, count), out_shape=tupl...  2.47 us

profile of v6, /device:TPU:0, one launch (start us, length us, event | category | flops | bytes accessed | tf_op | source)
XLA Modules:
  0.0 96.6 jit_solution(4249592386832800127)
XLA Ops:
  0.6 93.3 %shard_map.101 = (bf16[256,1024]{1,0:T(8,128)(2,1)}, bf16[256,1024]{1,0:T(8,128)(2,1)}, bf16[256,1024]{1,0:T(8,128)(2,1)}, bf16[256,1024]{1,0:T(8,128)(2,1)}, f32[32,1024]{1,0:T(8,128)}) custom-call(bf16[256,1024]{1,0:T(8,128)(2,1)} %bitcast.8, bf16[256,1024]{1,0:T(8,128)(2,1)} %bitcast.9, bf16[256,1024]{1,0:T(8,128)(2,1)} %bitcast.10, ...), custom_call_target="tpu_custom_call" | custom-call | tf_op jit(solution)/shard_map/pallas_call | solution.py:1058
  93.9 2.5 %shard_map.102 = (bf16[256,1024]{1,0:T(8,128)(2,1)}, bf16[256,1024]{1,0:T(8,128)(2,1)}, bf16[256,1024]{1,0:T(8,128)(2,1)}, bf16[256,1024]{1,0:T(8,128)(2,1)}, f32[32,1024]{1,0:T(8,128)}) custom-call(bf16[256,1024]{1,0:T(8,128)(2,1)} %get-tuple-element.15.refs_0_, bf16[256,1024]{1,0:T(8,128)(2,1)} %get-tuple-element.16.refs_1_, ...), custom_call_target="tpu_custom_call" | custom-call | tf_op jit(solution)/shard_map/pallas_call | solution.py:1090
